TPU v7x, 256 devices: a whole 4x4x8 slice. The times are simulated.
256 devices in a mesh: rows: 64 (over z, y, core), cols: 4 (over x).
Axes of the slice: x: 4, y: 4, z: 8, core: 2. Of those that a mesh axis runs over, the one named last changes fastest.
Arguments:
- cotangent: float32 [65536, 2048], P('rows', 'cols'), may hold values from -6 to 6
- saved: float32 [65536, 2048], P('rows', 'cols'), may hold values from -0.125 to 0.125
- panel: float32 [1024, 65536], P(None, 'rows'), may hold values from -0.25 to 0.25
- dinv: float32 [2, 512, 512], replicated, as said below
Outputs:
- cotangent_out: float32 [65536, 2048], P('rows', 'cols')
- factor_grad: float32 [2, 512, 65536], P(None, 'cols', 'rows')
Inputs may be any that keep to these rules, and one draw needn't show every extreme that they name: Each dinv[k] is lower triangular with a positive diagonal.
All inputs are finite; a program needn't handle non-finite values.
Results may differ from a plain program's by a relative error of at most 0.0001.
Values sent between devices are 32-bit elements; how exact they have to be, the bound alone decides.
No kernel may reach another device: no remote copies, remote signals or barrier semaphores. Data moves between devices by JAX's collectives and lax.ppermute only.
A program may use at most 64 MiB of HBM per device.

v0:
```python
import jax
import jax.numpy as jnp
from jax import lax
from jax.sharding import PartitionSpec as P

N = 65536
BS = 512
STEPS = 2


def on_device(cotangent, saved, panel, dinv):
    local_rows, local_cols = cotangent.shape
    row_rank = lax.axis_index("rows")
    first_row = row_rank * local_rows
    global_row = first_row + lax.broadcasted_iota(jnp.int32, (local_rows, 1), 0)
    column_global = first_row + lax.broadcasted_iota(jnp.int32, (1, local_rows), 1)
    window_start = N - STEPS * BS
    contract_lead = (((0,), (0,)), ((), ()))
    contract_last = (((1,), (1,)), ((), ()))
    highest = lax.Precision.HIGHEST
    carried = cotangent
    grad_parts = [None] * STEPS
    for k in range(STEPS - 1, -1, -1):
        block_start = window_start + k * BS
        zero_rows = jnp.zeros((BS, local_cols), jnp.float32)
        padded = jnp.concatenate([zero_rows, carried, zero_rows], 0)
        offset_in = jnp.clip(block_start - first_row + BS, 0, local_rows + BS)
        owned_rows = lax.dynamic_slice_in_dim(padded, offset_in, BS, 0)
        block_rows = lax.psum(owned_rows, "rows")
        solved = lax.dot_general(
            dinv[k],
            block_rows,
            contract_lead,
            precision=highest,
            preferred_element_type=jnp.float32,
        )
        update = lax.dot_general(
            panel[k * BS : (k + 1) * BS],
            solved,
            contract_lead,
            precision=highest,
            preferred_element_type=jnp.float32,
        )
        carried = jnp.where(global_row < block_start, carried - update, carried)
        zero_local = jnp.zeros((local_rows, local_cols), jnp.float32)
        solved_pad = jnp.concatenate([zero_local, solved, zero_local], 0)
        offset_out = jnp.clip(first_row - block_start + local_rows, 0, BS + local_rows)
        solved_rows = lax.dynamic_slice_in_dim(solved_pad, offset_out, local_rows, 0)
        inside = (global_row >= block_start) & (global_row < block_start + BS)
        carried = jnp.where(inside, solved_rows, carried)

        def grad_rows(row_first, row_count, solved=solved, block_start=block_start):
            product = lax.dot_general(
                solved, saved, contract_last, precision=highest, preferred_element_type=jnp.float32
            )
            limit = block_start + row_first + lax.broadcasted_iota(jnp.int32, (row_count, 1), 0)
            return jnp.where(column_global <= limit, -product, jnp.float32(0.0))

        grad_parts[k] = lax.psum_scatter(
            grad_rows(jnp.int32(0), lax.axis_size("cols") * (BS // lax.axis_size("cols"))),
            "cols",
            scatter_dimension=0,
            tiled=True,
        )
    stacked = jnp.stack(grad_parts, 0)
    return (carried, stacked)


def solution(mesh):
    return jax.shard_map(
        on_device,
        mesh=mesh,
        in_specs=(P("rows", "cols"), P("rows", "cols"), P(None, "rows"), P()),
        out_specs=(P("rows", "cols"), P(None, "cols", "rows")),
        check_vma=False,
    )
```

profile of v0, /device:TPU:1, one launch (start us, length us, event | category | flops | bytes accessed | tf_op | source)
XLA Modules:
  0.0 476.2 jit_solution(11177737984115424401)
XLA Ops:
  7.2 0.0 copy-start
  7.2 0.0 all-reduce.3.cloned.1.call-start
  7.2 0.1 broadcast.72.clone
  7.4 1.7 fusion.17
  9.1 0.0 all-reduce.3.cloned.1.call-update
  9.1 0.0 all-reduce.5.cloned.1.call-start
  9.1 2.9 copy.9
  12.0 187.6 %all-reduce.3.cloned.1.call-done = f32[512,512]{1,0:T(8,128)} async-done(((f32[512,512]{1,0:T(8,128)}), f32[512,512]{1,0:T(8,128)}) %all-reduce.3.cloned.1.call-update) | async-done | bytes 1048592 | tf_op jit(solution)/shard_map/psum | solution.py:29
  199.6 3.4 fusion.20
  203.1 1.3 copy.8
  204.4 0.0 copy-start.3
  204.4 0.2 broadcast.71
  204.6 1.3 copy-done.3
  206.0 0.0 copy-start.1
  206.0 6.3 %fusion = f32[1024,512]{0,1:T(8,128)S(1)} fusion(f32[1024,512]{0,1:T(8,128)S(1)} %copy-done.3, s32[]{:T(128)S(6)} %min.14, f32[512,512]{0,1:T(8,128)} %copy.8, f32[1024,512]{0,1:T(8,128)S(1)} %broadcast.71, f32[512,512]{0,1:T(8,128)S(1)} %fusion.20, f32[1024,1024]{1,0:T(8,128)} %param.6, pred[1024]{0:T(1024)(128)(4,1)S(1)} %get-tuple-element.6, ...), kind=kOutput, calls=%fused_computation.14 | convolution fusion | flops 3223846912 | bytes 10487812 | tf_op jit(solution)/shard_map/dot_general | solution.py:37
  212.3 0.0 copy-done.1
  212.3 0.0 copy-start.2
  212.3 0.1 broadcast.72
  212.4 1.2 copy-done.2
  213.6 1.9 fusion.15
  215.5 0.0 all-reduce.5.cloned.1.call-update
  215.5 0.2 reduce-scatter.5.cloned.1.call-start
  215.7 0.0 copy-done
  215.7 4.9 %negate_select_fusion = f32[512,1024]{1,0:T(8,128)} fusion(f32[512,512]{0,1:T(8,128)S(1)} %fusion.20, f32[1024,512]{1,0:T(8,128)S(1)} %copy-done, s32[1024]{0:T(1024)S(1)} %iota_add_fusion, s32[512]{0:T(512)S(1)} %iota_add_fusion.1), kind=kOutput, calls=%fused_computation.20 | convolution fusion | flops 3222798336 | bytes 5249024 | tf_op jit(solution)/shard_map/dot_general | solution.py:53
  220.6 0.0 reduce-scatter.5.cloned.1.call-update
  220.7 0.0 reduce-scatter.3.cloned.1.call-start
  220.7 178.1 %all-reduce.5.cloned.1.call-done = f32[512,512]{0,1:T(8,128)} async-done(((f32[512,512]{0,1:T(8,128)}), f32[512,512]{0,1:T(8,128)}) %all-reduce.5.cloned.1.call-update) | async-done | bytes 1048592 | tf_op jit(solution)/shard_map/psum | solution.py:29
  398.8 3.4 fusion.18
  402.3 4.9 %negate_select_fusion.1 = f32[512,1024]{1,0:T(8,128)} fusion(f32[512,512]{0,1:T(8,128)S(1)} %fusion.18, f32[1024,512]{1,0:T(8,128)S(1)} %copy-done, s32[1024]{0:T(1024)S(1)} %iota_add_fusion, s32[512]{0:T(512)S(1)} %iota_add_fusion.2), kind=kOutput, calls=%fused_computation.21 | convolution fusion | flops 3222798336 | bytes 5249024 | tf_op jit(solution)/shard_map/dot_general | solution.py:53
  407.2 0.0 reduce-scatter.3.cloned.1.call-update
  407.2 1.3 copy.11
  408.5 7.4 %fusion.1 = f32[1024,512]{0,1:T(8,128)} fusion(f32[1024,512]{0,1:T(8,128)} %copy-done.2, s32[]{:T(128)S(6)} %min.16, f32[512,512]{0,1:T(8,128)} %bitcast.23, f32[1024,512]{0,1:T(8,128)} %copy-done.1, f32[512,512]{0,1:T(8,128)S(1)} %fusion.18, f32[1024,1024]{1,0:T(8,128)} %param.6, pred[1024]{0:T(1024)(128)(4,1)S(1)} %get-tuple-element.4, ...), kind=kOutput, calls=%fused_computation.15 | convolution fusion | flops 3223846912 | bytes 10487812 | tf_op jit(solution)/shard_map/dot_general | solution.py:37
  415.9 2.9 copy.12
  418.8 14.0 %reduce-scatter.5.cloned.1.call-done = f32[128,1024]{1,0:T(8,128)} async-done(((f32[512,1024]{1,0:T(8,128)}), f32[128,1024]{1,0:T(8,128)}) %reduce-scatter.5.cloned.1.call-update) | async-done | bytes 524304 | tf_op jit(solution)/shard_map/reduce_scatter | solution.py:59
  432.8 34.6 %reduce-scatter.3.cloned.1.call-done = f32[128,1024]{1,0:T(8,128)} async-done(((f32[512,1024]{1,0:T(8,128)}), f32[128,1024]{1,0:T(8,128)}) %reduce-scatter.3.cloned.1.call-update) | async-done | bytes 524304 | tf_op jit(solution)/shard_map/reduce_scatter | solution.py:59
  467.4 2.3 pad_maximum_fusion
  (5 shorter events, 0.0 us)
Async XLA Ops:
  7.2 208.6 %copy-start = (f32[1024,512]{1,0:T(8,128)S(1)}, f32[1024,512]{1,0:T(8,128)}, u32[]{:S(2)}) copy-start(f32[1024,512]{1,0:T(8,128)} %param.5) | copy-start | bytes 6291460
  7.2 192.5 %all-reduce.3.cloned.1.call-start = ((), (), s32[]{:S(2)}) async-start(), calls=%async_computation.2 | async-start | bytes 2097152 | tf_op jit(solution)/shard_map/psum | solution.py:29
  9.1 389.8 %all-reduce.5.cloned.1.call-start = ((), (), s32[]{:S(2)}) async-start(), calls=%async_computation.3 | async-start | bytes 2097152 | tf_op jit(solution)/shard_map/psum | solution.py:29
  204.4 1.6 copy-start.3
  206.0 6.3 %copy-start.1 = (f32[1024,512]{0,1:T(8,128)}, f32[1024,512]{0,1:T(8,128)S(1)}, u32[]{:S(2)}) copy-start(f32[1024,512]{0,1:T(8,128)S(1)} %broadcast.71) | copy-start | bytes 6291460
  212.3 1.3 copy-start.2
  215.5 217.3 %reduce-scatter.5.cloned.1.call-start = ((), (), s32[]{:S(2)}) async-start(), calls=%async_computation.5 | async-start | bytes 2621440 | tf_op jit(solution)/shard_map/reduce_scatter | solution.py:59
  220.7 246.7 %reduce-scatter.3.cloned.1.call-start = ((), (), s32[]{:S(2)}) async-start(), calls=%async_computation.4 | async-start | bytes 2621440 | tf_op jit(solution)/shard_map/reduce_scatter | solution.py:59
Sparse Core Ops, SparseCore 0:
  12.0 187.5 all-reduce.2
  215.6 183.1 all-reduce.4
  401.4 31.3 reduce-scatter.4
  435.4 31.9 reduce-scatter.2
where the time goes:
time: 476 us
  waiting for transfers between devices  414 us (87%)
  matrix products  30.3 us (6%)
  between operations  13.9 us (3%)
  local copies, waits for them, and re-layouts  11.4 us (2%)
  other arithmetic  5.86 us (1%)
    psum x2, waiting for transfers between devices, on_device(): block_rows = lax.psum(owned_rows, 'rows')  366 us
    reduce_scatter x2, waiting for transfers between devices, on_device(): lax.psum_scatter(grad_rows(jnp.int32(0), lax.axis_size('cols') * (BS // l...  48.6 us
    dot_general x2, matrix products, on_device(): lax.dot_general(panel[k * BS:(k + 1) * BS], solved, contract_lead, precis...  13.7 us
    dot_general x2, matrix products, grad_rows(): lax.dot_general(solved, saved, contract_last, precision=highest, preferre...  9.79 us
  transfers between devices with their start and end apart: 4, of which 4 were waited for; matrix products, arithmetic and copies ran while one was open for 6% of the time, Pallas kernels for 0%

commit v1 on v0

v1 whole, which is shorter than its diff:
```python
import jax
import jax.numpy as jnp
from jax import lax
from jax.sharding import PartitionSpec as P

STEPS = 2
LEAD = (((0,), (0,)), ((), ()))
LAST = (((1,), (1,)), ((), ()))
NZ, NY, NX = 8, 4, 4
ROOT_Z, ROOT_Y = NZ - 1, NY - 1


def rank(z, y, c):
    return ((z % NZ) * NY + y % NY) * 2 + c


def carrier(z):
    return 0 if z in (4, 5, 6) else 1


ROOT = rank(ROOT_Z, ROOT_Y, 1)
SWAP = [(r, r ^ 1) for r in range(NZ * NY * 2)]
Y_SCATTER = [[(ROOT, rank(ROOT_Z, ROOT_Y + i, 1))] for i in range(1, NY)]
Z_SEND = [
    [(rank(ROOT_Z, y, 1), rank(ROOT_Z + d, y, 1)) for y in range(NY)]
    + [(rank(ROOT_Z, y, 0), rank(ROOT_Z - d, y, 0)) for y in range(NY) if d < 4]
    for d in (4, 3, 2, 1)
]
Y_SHIFT = [
    [(rank(z, y, carrier(z)), rank(z, y + s, carrier(z))) for z in range(NZ) for y in range(NY)]
    for s in range(1, NY)
]
X_RIGHT = [(q, (q + 1) % NX) for q in range(NX)]
X_LEFT = [(q, (q - 1) % NX) for q in range(NX)]


def dot(a, b, dims):
    return lax.dot_general(a, b, dims, precision=lax.Precision.HIGH, preferred_element_type=jnp.float32)


def on_device(cotangent, saved, panel, dinv):
    bs = dinv.shape[1]
    quarter = bs // 4
    half = quarter // 2
    me = lax.axis_index("rows")
    q = lax.axis_index("cols")
    z, y, c = me // (2 * NY), (me // 2) % NY, me % 2
    is_root = me == ROOT
    in_root_z = z == ROOT_Z
    is_carrier = c == jnp.where((z >= 4) & (z <= 6), 0, 1)
    mine = (y - ROOT_Y) % NY

    def rows(x, perm):
        return lax.ppermute(x, "rows", perm)

    def broadcast(x):
        parts = [x[i * quarter : (i + 1) * quarter] for i in range(4)]
        got = [rows(parts[i + 1], Y_SCATTER[i]) for i in range(3)]
        piece = jnp.where(is_root, parts[0], got[0] + got[1] + got[2])
        other = rows(piece, SWAP)
        piece = jnp.where(c == 1, piece, other)
        sent = [rows(piece, p) for p in Z_SEND]
        piece = jnp.where(in_root_z, piece, sent[0] + sent[1] + sent[2] + sent[3])
        back = [rows(piece, p) for p in Y_SHIFT]
        whole = jnp.concatenate([piece, back[2], back[1], back[0]], 0)
        other = rows(whole, SWAP)
        return jnp.where(is_carrier, whole, other)

    def turned(x, by):
        twice = jnp.concatenate([x, x], 0)
        return lax.dynamic_slice_in_dim(twice, by * quarter, bs, 0)

    def gradient(k, cyclic):
        from_q = turned(cyclic, (q - mine) % 4)
        a, b = quarter + half, 2 * quarter + half
        to_right = dot(from_q[a:b], saved, LAST)
        to_left = dot(from_q[b : b + quarter], saved, LAST)
        left1 = lax.ppermute(to_right, "cols", X_RIGHT)
        right1 = lax.ppermute(to_left, "cols", X_LEFT)
        next_a = dot(from_q[quarter:a], saved, LAST)
        prev_b = dot(from_q[b + quarter :], saved, LAST)
        own = dot(from_q[:quarter], saved, LAST)
        left2 = lax.ppermute(next_a + left1[half:], "cols", X_RIGHT)
        right2 = lax.ppermute(prev_b + right1[:half], "cols", X_LEFT)
        total = jnp.concatenate(
            [own[:half] + right1[half:] + left2, own[half:] + left1[:half] + right2], 0
        )
        first = me * cotangent.shape[0]
        start = NZ * NY * 2 * cotangent.shape[0] - STEPS * bs + k * bs
        limit = start + q * quarter + lax.broadcasted_iota(jnp.int32, (quarter, 1), 0)
        column = first + lax.broadcasted_iota(jnp.int32, (1, cotangent.shape[0]), 1)
        return jnp.where(column <= limit, -total, jnp.float32(0.0))

    local1 = dot(dinv[1], cotangent[bs:], LEAD)
    cyclic1 = broadcast(local1)
    local0 = dot(dinv[0], cotangent[:bs] - dot(panel[bs:, :bs], local1, LEAD), LEAD)
    cyclic0 = broadcast(local0)
    grad1 = gradient(1, cyclic1)
    grad0 = gradient(0, cyclic0)
    update = dot(panel[bs:], turned(cyclic1, (-mine) % 4), LEAD)
    update += dot(panel[:bs], turned(cyclic0, (-mine) % 4), LEAD)
    carried = jnp.where(is_root, jnp.concatenate([local0, local1], 0), cotangent - update)
    return carried, jnp.stack([grad0, grad1], 0)


def solution(mesh):
    return jax.shard_map(
        on_device,
        mesh=mesh,
        in_specs=(P("rows", "cols"), P("rows", "cols"), P(None, "rows"), P()),
        out_specs=(P("rows", "cols"), P(None, "cols", "rows")),
        check_vma=False,
    )
```

time: 476 us -> 139 us (0.29)
  waiting for transfers between devices: 414 us -> 45.2 us
  starting transfers between devices: 0.34 us -> 51.3 us
  between operations: 13.9 us -> 1.27 us
  local copies, waits for them, and re-layouts: 11.4 us -> 2.83 us
  matrix products: 30.3 us -> 22.9 us
  other arithmetic: 5.86 us -> 12.7 us
    psum x2 -> x0, waiting for transfers between devices: 366 us -> none  [on_device(): block_rows = lax.psum(owned_rows, 'rows')]
    ppermute x0 -> x32, starting transfers between devices: none -> 51.3 us  [the longest x24 39 us: rows(): return lax.ppermute(x, 'rows', perm)]
    reduce_scatter x2 -> x0, waiting for transfers between devices: 48.6 us -> none  [on_device(): lax.psum_scatter(grad_rows(jnp.int32(0), lax.axis_size('cols') * (BS // l...]
    ppermute x0 -> x32, waiting for transfers between devices: none -> 45.2 us  [the longest x24 32.5 us: rows(): return lax.ppermute(x, 'rows', perm)]
    dot_general x6 -> x15, matrix products: 30.3 us -> 22.9 us  [dot(): lax.dot_general(a, b, dims, precision=lax.Precision.HIGH, preferred_eleme...]
    select_n x0 -> x9, other arithmetic: none -> 7.35 us  [the longest x2 2.73 us: broadcast(): return jnp.where(is_carrier, whole, other)]
    unnamed x10 -> x20, local copies, waits for them, and re-layouts: 8.31 us -> 1.02 us
  transfers between devices with their start and end apart: 4 -> 32, of which waited for: 4 -> 9; matrix products, arithmetic and copies ran while one was open for 6% -> 20% of each run, Pallas kernels for 0% -> 0%
where the time goes in v1:
time: 139 us; the launch traced here: 136 us
  starting transfers between devices  51.3 us (37%)
  waiting for transfers between devices  45.2 us (33%)
  matrix products  22.9 us (16%)
  other arithmetic  12.7 us (9%)
  local copies, waits for them, and re-layouts  2.83 us (2%)
    ppermute x24, starting transfers between devices, rows(): return lax.ppermute(x, 'rows', perm)  39 us
    ppermute x24, waiting for transfers between devices, rows(): return lax.ppermute(x, 'rows', perm)  32.5 us
    dot_general x15, matrix products, dot(): lax.dot_general(a, b, dims, precision=lax.Precision.HIGH, preferred_eleme...  22.9 us
    ppermute x2, starting transfers between devices, gradient(): right2 = lax.ppermute(prev_b + right1[:half], 'cols', X_LEFT)  6.85 us
    ppermute x2, waiting for transfers between devices, gradient(): right1 = lax.ppermute(to_left, 'cols', X_LEFT)  5.49 us
    ppermute x2, starting transfers between devices, gradient(): right1 = lax.ppermute(to_left, 'cols', X_LEFT)  5.23 us
    ppermute x2, waiting for transfers between devices, gradient(): left2 = lax.ppermute(next_a + left1[half:], 'cols', X_RIGHT)  5.12 us
    concatenate x2, other arithmetic, broadcast(): whole = jnp.concatenate([piece, back[2], back[1], back[0]], 0)  3.27 us
  transfers between devices with their start and end apart: 32, of which 9 were waited for; matrix products, arithmetic and copies ran while one was open for 20% of the time, Pallas kernels for 0%

profile of v1, /device:TPU:1, one launch (start us, length us, event | category | flops | bytes accessed | tf_op | source)
XLA Modules:
  0.0 136.2 jit_solution(8594411960395925922)
XLA Ops:
  0.6 2.7 %fusion.14 = f32[512,512]{1,0:T(8,128)S(1)} fusion(f32[1024,512]{1,0:T(8,128)} %param.4, f32[2,512,512]{2,1,0:T(8,128)} %param.7), kind=kOutput, calls=%fused_computation.25 | convolution fusion | flops 805306368 | bytes 3145728 | tf_op jit(solution)/shard_map/dot_general | solution.py:38
  3.4 0.9 fusion.62
  4.3 0.7 collective-permute-start
  4.9 1.4 %collective-permute-start.1 = (f32[128,512]{1,0:T(8,128)}, f32[128,512]{1,0:T(8,128)}, u32[]{:S(2)}, u32[]{:S(2)}) collective-permute-start(f32[128,512]{1,0:T(8,128)} %get-tuple-element.2), channel_id=1, source_target_pairs={{252,236},{253,237},{254,238},{255,239}} | collective-permute-start | bytes 786440 | tf_op jit(solution)/shard_map/ppermute | solution.py:54
  6.3 1.4 %collective-permute-start.2 = (f32[128,512]{1,0:T(8,128)}, f32[128,512]{1,0:T(8,128)}, u32[]{:S(2)}, u32[]{:S(2)}) collective-permute-start(f32[128,512]{1,0:T(8,128)} %get-tuple-element.3), channel_id=1, source_target_pairs={{252,244},{253,245},{254,246},{255,247}} | collective-permute-start | bytes 786440 | tf_op jit(solution)/shard_map/ppermute | solution.py:54
  7.7 1.1 slice_select_fusion.1
  8.8 3.3 %collective-permute-start.3 = (f32[128,512]{1,0:T(8,128)S(1)}, f32[128,512]{1,0:T(8,128)S(1)}, u32[]{:S(2)}, u32[]{:S(2)}) collective-permute-start(f32[128,512]{1,0:T(8,128)S(1)} %slice_select_fusion.1), channel_id=1, source_target_pairs={{0,4},{4,0},{8,12},{12,8},{16,20},{20,16},{24,28},{28,24},{32,36},... | collective-permute-start | bytes 786440 | tf_op jit(solution)/shard_map/ppermute | solution.py:54
  12.2 2.6 %fusion.6 = f32[512,512]{1,0:T(8,128)S(1)} fusion(f32[512,512]{1,0:T(8,128)S(1)} %fusion.14, f32[1024,1024]{1,0:T(8,128)} %param.6, f32[1024,512]{1,0:T(8,128)} %param.4), kind=kOutput, calls=%fused_computation.16 | convolution fusion | flops 805568512 | bytes 4194304 | tf_op jit(solution)/shard_map/dot_general | solution.py:38
  14.8 1.4 %collective-permute-start.4 = (f32[128,512]{1,0:T(8,128)S(1)}, f32[128,512]{1,0:T(8,128)}, u32[]{:S(2)}, u32[]{:S(2)}) collective-permute-start(f32[128,512]{1,0:T(8,128)S(1)} %broadcast_select_fusion.3), channel_id=1, source_target_pairs={{228,100},{236,108},{244,116},{252,124},{229,101},{237,109},{245,1... | collective-permute-start | bytes 786440 | tf_op jit(solution)/shard_map/ppermute | solution.py:54
  16.2 1.4 collective-permute-start.5
  17.5 1.4 %collective-permute-start.6 = (f32[128,512]{1,0:T(8,128)S(1)}, f32[128,512]{1,0:T(8,128)}, u32[]{:S(2)}, u32[]{:S(2)}) collective-permute-start(f32[128,512]{1,0:T(8,128)S(1)} %broadcast_select_fusion.3), channel_id=1, source_target_pairs={{228,36},{236,44},{244,52},{252,60},{224,160},{232,168},{240,176},... | collective-permute-start | bytes 786440 | tf_op jit(solution)/shard_map/ppermute | solution.py:54
  18.9 1.3 collective-permute-start.7
  20.2 1.0 convolution_bitcast_fusion
  21.3 1.0 copy-done.1
  22.2 0.9 fusion.63
  23.1 1.4 %collective-permute-start.12 = (f32[128,512]{1,0:T(8,128)}, f32[128,512]{1,0:T(8,128)}, u32[]{:S(2)}, u32[]{:S(2)}) collective-permute-start(f32[128,512]{1,0:T(8,128)} %get-tuple-element.7), channel_id=1, source_target_pairs={{252,228},{253,229},{254,230},{255,231}} | collective-permute-start | bytes 786440 | tf_op jit(solution)/shard_map/ppermute | solution.py:54
  24.5 0.7 collective-permute-start.13
  25.2 0.7 collective-permute-start.14
  25.9 10.0 %collective-permute-done.7 = f32[128,512]{1,0:T(8,128)} collective-permute-done((f32[128,512]{1,0:T(8,128)S(1)}, f32[128,512]{1,0:T(8,128)}, u32[]{:S(2)}, u32[]{:S(2)}) %collective-permute-start.7) | collective-permute-done | bytes 262176 | tf_op jit(solution)/shard_map/ppermute | solution.py:54
  36.0 1.3 add_select_fusion.1
  37.3 4.3 %collective-permute-start.10 = (f32[128,512]{1,0:T(8,128)S(1)}, f32[128,512]{1,0:T(8,128)S(1)}, u32[]{:S(2)}, u32[]{:S(2)}) collective-permute-start(f32[128,512]{1,0:T(8,128)S(1)} %add_select_fusion.1), channel_id=1, source_target_pairs={{4,12},{12,20},{20,28},{28,4},{36,44},{44,52},{52,60},{60,36},{68,... | collective-permute-start | bytes 786440 | tf_op jit(solution)/shard_map/ppermute | solution.py:54
  41.6 3.7 %collective-permute-start.8 = (f32[128,512]{1,0:T(8,128)S(1)}, f32[128,512]{1,0:T(8,128)S(1)}, u32[]{:S(2)}, u32[]{:S(2)}) collective-permute-start(f32[128,512]{1,0:T(8,128)S(1)} %add_select_fusion.1), channel_id=1, source_target_pairs={{4,28},{12,4},{20,12},{28,20},{36,60},{44,36},{52,44},{60,52},{68,... | collective-permute-start | bytes 786440 | tf_op jit(solution)/shard_map/ppermute | solution.py:54
  45.3 5.0 %collective-permute-start.9 = (f32[128,512]{1,0:T(8,128)S(1)}, f32[128,512]{1,0:T(8,128)S(1)}, u32[]{:S(2)}, u32[]{:S(2)}) collective-permute-start(f32[128,512]{1,0:T(8,128)S(1)} %add_select_fusion.1), channel_id=1, source_target_pairs={{4,20},{12,28},{20,4},{28,12},{36,52},{44,60},{52,36},{60,44},{68,... | collective-permute-start | bytes 786440 | tf_op jit(solution)/shard_map/ppermute | solution.py:54
  50.3 1.1 slice_select_fusion
  51.6 2.4 %collective-permute-done.9 = f32[128,512]{1,0:T(8,128)S(1)} collective-permute-done((f32[128,512]{1,0:T(8,128)S(1)}, f32[128,512]{1,0:T(8,128)S(1)}, u32[]{:S(2)}, u32[]{:S(2)}) %collective-permute-start.9) | collective-permute-done | bytes 262176 | tf_op jit(solution)/shard_map/ppermute | solution.py:54
  54.0 1.0 pad_maximum_fusion
  55.1 0.7 collective-permute-start.16
  55.8 0.7 collective-permute-start.17
  56.5 0.7 collective-permute-start.18
  57.2 1.3 collective-permute-start.19
  58.5 12.6 %collective-permute-done.19 = f32[128,512]{1,0:T(8,128)S(1)} collective-permute-done((f32[128,512]{1,0:T(8,128)S(1)}, f32[128,512]{1,0:T(8,128)S(1)}, u32[]{:S(2)}, u32[]{:S(2)}) %collective-permute-start.19) | collective-permute-done | bytes 262176 | tf_op jit(solution)/shard_map/ppermute | solution.py:54
  71.1 0.8 add_select_fusion
  72.0 3.4 %collective-permute-start.20 = (f32[128,512]{1,0:T(8,128)}, f32[128,512]{1,0:T(8,128)}, u32[]{:S(2)}, u32[]{:S(2)}) collective-permute-start(f32[128,512]{1,0:T(8,128)} %add_select_fusion), channel_id=1, source_target_pairs={{4,28},{12,4},{20,12},{28,20},{36,60},{44,36},{52,44},{60,52},{68,... | collective-permute-start | bytes 786440 | tf_op jit(solution)/shard_map/ppermute | solution.py:54
  75.3 2.2 %collective-permute-start.21 = (f32[128,512]{1,0:T(8,128)}, f32[128,512]{1,0:T(8,128)}, u32[]{:S(2)}, u32[]{:S(2)}) collective-permute-start(f32[128,512]{1,0:T(8,128)} %add_select_fusion), channel_id=1, source_target_pairs={{4,20},{12,28},{20,4},{28,12},{36,52},{44,60},{52,36},{60,44},{68,... | collective-permute-start | bytes 786440 | tf_op jit(solution)/shard_map/ppermute | solution.py:54
  77.5 2.2 %collective-permute-start.22 = (f32[128,512]{1,0:T(8,128)}, f32[128,512]{1,0:T(8,128)}, u32[]{:S(2)}, u32[]{:S(2)}) collective-permute-start(f32[128,512]{1,0:T(8,128)} %add_select_fusion), channel_id=1, source_target_pairs={{4,12},{12,20},{20,28},{28,4},{36,44},{44,52},{52,60},{60,36},{68,... | collective-permute-start | bytes 786440 | tf_op jit(solution)/shard_map/ppermute | solution.py:54
  79.8 4.6 %collective-permute-done.21 = f32[128,512]{1,0:T(8,128)} collective-permute-done((f32[128,512]{1,0:T(8,128)}, f32[128,512]{1,0:T(8,128)}, u32[]{:S(2)}, u32[]{:S(2)}) %collective-permute-start.21) | collective-permute-done | bytes 262176 | tf_op jit(solution)/shard_map/ppermute | solution.py:54
  84.4 2.7 %collective-permute-done.22 = f32[128,512]{1,0:T(8,128)} collective-permute-done((f32[128,512]{1,0:T(8,128)}, f32[128,512]{1,0:T(8,128)}, u32[]{:S(2)}, u32[]{:S(2)}) %collective-permute-start.22) | collective-permute-done | bytes 262176 | tf_op jit(solution)/shard_map/ppermute | solution.py:54
  87.1 2.2 %pad_maximum_fusion.1 = f32[512,512]{1,0:T(8,128)} fusion(f32[128,512]{1,0:T(8,128)} %collective-permute-done.22, f32[128,512]{1,0:T(8,128)} %collective-permute-done.21, f32[128,512]{1,0:T(8,128)} %collective-permute-done.20, f32[128,512]{1,0:T(8,128)} %add_select_fusion), kind=kLoop, calls=%fused_computation.22 | loop fusion | flops 786432 | bytes 2097152 | tf_op jit(solution)/shard_map/concatenate | solution.py:65
  89.4 1.3 broadcast_select_fusion.1
  90.8 0.4 fusion.10
  91.2 1.2 fusion.28
  92.4 1.2 fusion.24
  93.6 1.4 %broadcast_select_fusion = f32[512,512]{1,0:T(8,128)S(1)} fusion(f32[512,512]{1,0:T(8,128)} %collective-permute-done.23, pred[]{:T(512)S(6)} %eq.22, f32[128,512]{1,0:T(8,128)} %collective-permute-done.22, f32[128,512]{1,0:T(8,128)} %collective-permute-done.21, f32[128,512]{1,0:T(8,128)} %collective-permute-done.20, f32[128,512]{1,0:T(8,128)} %add_select_fusion), kind=kLoop, calls=%fused_computation.35 | loop fusion | flops 1048576 | bytes 3145729 | tf_op jit(solution)/shard_map/jit(_where)/select_n | solution.py:67
  95.0 0.4 fusion.7
  95.4 1.2 fusion.38
  96.6 1.2 fusion.34
  97.8 2.6 %collective-permute-start.28 = (f32[128,1024]{1,0:T(8,128)S(1)}, f32[128,1024]{1,0:T(8,128)S(1)}, u32[]{:S(2)}, u32[]{:S(2)}) collective-permute-start(f32[128,1024]{1,0:T(8,128)S(1)} %fusion.28), channel_id=1, source_target_pairs={{0,3},{1,0},{2,1},{3,2},{4,7},{5,4},{6,5},{7,6},{8,11},{9,8},{10,9... | collective-permute-start | bytes 1572872 | tf_op jit(solution)/shard_map/ppermute | solution.py:79
  100.4 2.7 %collective-permute-start.24 = (f32[128,1024]{1,0:T(8,128)S(1)}, f32[128,1024]{1,0:T(8,128)S(1)}, u32[]{:S(2)}, u32[]{:S(2)}) collective-permute-start(f32[128,1024]{1,0:T(8,128)S(1)} %fusion.38), channel_id=1, source_target_pairs={{0,3},{1,0},{2,1},{3,2},{4,7},{5,4},{6,5},{7,6},{8,11},{9,8},{10,9... | collective-permute-start | bytes 1572872 | tf_op jit(solution)/shard_map/ppermute | solution.py:79
  103.0 1.9 %fusion = f32[512,1024]{0,1:T(8,128)S(1)} fusion(f32[1024,1024]{1,0:T(8,128)S(1)} %copy-done.4, s32[]{:T(128)S(6)} %select_n.135, f32[512,512]{1,0:T(8,128)S(1)} %broadcast_select_fusion), kind=kOutput, calls=%fused_computation.10 | convolution fusion | flops 1610874880 | bytes 5242884 | tf_op jit(solution)/shard_map/dot_general | solution.py:38
  105.0 3.3 %maximum_select_fusion = f32[1024,512]{1,0:T(8,128)} fusion(f32[512,512]{1,0:T(8,128)S(1)} %fusion.14, f32[512,512]{1,0:T(8,128)S(1)} %copy-done.2, f32[1024,512]{1,0:T(8,128)S(1)} %copy-done.3, f32[512,1024]{0,1:T(8,128)S(1)} %fusion, f32[1024,1024]{1,0:T(8,128)S(1)} %copy-done.4, s32[]{:T(128)S(6)} %select_n.135, ...), kind=kOutput, calls=%fused_computation.8 | convolution fusion | flops 1612972032 | bytes 11534341 | tf_op jit(solution)/shard_map/dot_general | solution.py:38
  108.3 1.2 fusion.30
  109.5 1.2 fusion.40
  110.7 1.1 slice_add_fusion
  111.8 3.4 %collective-permute-start.31 = (f32[64,1024]{1,0:T(8,128)S(1)}, f32[64,1024]{1,0:T(8,128)S(1)}, u32[]{:S(2)}, u32[]{:S(2)}) collective-permute-start(f32[64,1024]{1,0:T(8,128)S(1)} %slice_add_fusion), channel_id=1, source_target_pairs={{0,3},{1,0},{2,1},{3,2},{4,7},{5,4},{6,5},{7,6},{8,11},{9,8},{10,9... | collective-permute-start | bytes 786440 | tf_op jit(solution)/shard_map/ppermute | solution.py:84
  115.1 1.1 slice_add_fusion.2
  116.3 5.5 %collective-permute-done.24 = f32[128,1024]{1,0:T(8,128)S(1)} collective-permute-done((f32[128,1024]{1,0:T(8,128)S(1)}, f32[128,1024]{1,0:T(8,128)S(1)}, u32[]{:S(2)}, u32[]{:S(2)}) %collective-permute-start.24) | collective-permute-done | bytes 524320 | tf_op jit(solution)/shard_map/ppermute | solution.py:79
  121.8 1.1 slice_add_fusion.4
  122.9 3.5 %collective-permute-start.27 = (f32[64,1024]{1,0:T(8,128)S(1)}, f32[64,1024]{1,0:T(8,128)S(1)}, u32[]{:S(2)}, u32[]{:S(2)}) collective-permute-start(f32[64,1024]{1,0:T(8,128)S(1)} %slice_add_fusion.4), channel_id=1, source_target_pairs={{0,3},{1,0},{2,1},{3,2},{4,7},{5,4},{6,5},{7,6},{8,11},{9,8},{10,9... | collective-permute-start | bytes 786440 | tf_op jit(solution)/shard_map/ppermute | solution.py:84
  126.4 1.1 slice_add_fusion.6
  127.6 3.0 %collective-permute-done.30 = f32[64,1024]{1,0:T(8,128)S(1)} collective-permute-done((f32[64,1024]{1,0:T(8,128)S(1)}, f32[64,1024]{1,0:T(8,128)S(1)}, u32[]{:S(2)}, u32[]{:S(2)}) %collective-permute-start.30) | collective-permute-done | bytes 262176 | tf_op jit(solution)/shard_map/ppermute | solution.py:83
  130.6 2.1 %collective-permute-done.27 = f32[64,1024]{1,0:T(8,128)S(1)} collective-permute-done((f32[64,1024]{1,0:T(8,128)S(1)}, f32[64,1024]{1,0:T(8,128)S(1)}, u32[]{:S(2)}, u32[]{:S(2)}) %collective-permute-start.27) | collective-permute-done | bytes 262176 | tf_op jit(solution)/shard_map/ppermute | solution.py:84
  132.8 2.1 %collective-permute-done.26 = f32[64,1024]{1,0:T(8,128)S(1)} collective-permute-done((f32[64,1024]{1,0:T(8,128)S(1)}, f32[64,1024]{1,0:T(8,128)S(1)}, u32[]{:S(2)}, u32[]{:S(2)}) %collective-permute-start.26) | collective-permute-done | bytes 262176 | tf_op jit(solution)/shard_map/ppermute | solution.py:83
  135.0 0.2 fusion.20
  135.2 1.1 pad_maximum_fusion.2
  (55 shorter events, 0.6 us)
Async XLA Ops:
  0.6 90.6 %copy-start = (f32[1024,512]{1,0:T(8,128)S(1)}, f32[1024,512]{1,0:T(8,128)}, u32[]{:S(2)}) copy-start(f32[1024,512]{1,0:T(8,128)} %param.5) | copy-start | bytes 6291460
  4.3 3.4 %collective-permute-start = (f32[128,512]{1,0:T(8,128)}, f32[128,512]{1,0:T(8,128)S(1)}, u32[]{:S(2)}, u32[]{:S(2)}) collective-permute-start(f32[128,512]{1,0:T(8,128)} %get-tuple-element.4), channel_id=1, source_target_pairs={{252,228},{253,229},{254,230},{255,231}} | collective-permute-start | bytes 786440 | tf_op jit(solution)/shard_map/ppermute | solution.py:54
  4.9 2.8 %collective-permute-start.1 = (f32[128,512]{1,0:T(8,128)}, f32[128,512]{1,0:T(8,128)}, u32[]{:S(2)}, u32[]{:S(2)}) collective-permute-start(f32[128,512]{1,0:T(8,128)} %get-tuple-element.2), channel_id=1, source_target_pairs={{252,236},{253,237},{254,238},{255,239}} | collective-permute-start | bytes 786440 | tf_op jit(solution)/shard_map/ppermute | solution.py:54
  6.3 1.4 %collective-permute-start.2 = (f32[128,512]{1,0:T(8,128)}, f32[128,512]{1,0:T(8,128)}, u32[]{:S(2)}, u32[]{:S(2)}) collective-permute-start(f32[128,512]{1,0:T(8,128)} %get-tuple-element.3), channel_id=1, source_target_pairs={{252,244},{253,245},{254,246},{255,247}} | collective-permute-start | bytes 786440 | tf_op jit(solution)/shard_map/ppermute | solution.py:54
  8.8 11.4 %copy-start.5 = (f32[2,512,512]{2,1,0:T(8,128)S(1)}, f32[2,512,512]{2,1,0:T(8,128)}, u32[]{:S(2)}) copy-start(f32[2,512,512]{2,1,0:T(8,128)} %param.7) | copy-start | bytes 6291460
  8.8 5.9 %collective-permute-start.3 = (f32[128,512]{1,0:T(8,128)S(1)}, f32[128,512]{1,0:T(8,128)S(1)}, u32[]{:S(2)}, u32[]{:S(2)}) collective-permute-start(f32[128,512]{1,0:T(8,128)S(1)} %slice_select_fusion.1), channel_id=1, source_target_pairs={{0,4},{4,0},{8,12},{12,8},{16,20},{20,16},{24,28},{28,24},{32,36},... | collective-permute-start | bytes 786440 | tf_op jit(solution)/shard_map/ppermute | solution.py:54
  14.8 8.3 %copy-start.6 = (f32[128,512]{1,0:T(8,128)}, f32[128,512]{1,0:T(8,128)S(1)}, u32[]{:S(2)}) copy-start(f32[128,512]{1,0:T(8,128)S(1)} %broadcast_select_fusion.3) | copy-start | bytes 786436
  14.8 9.7 %collective-permute-start.4 = (f32[128,512]{1,0:T(8,128)S(1)}, f32[128,512]{1,0:T(8,128)}, u32[]{:S(2)}, u32[]{:S(2)}) collective-permute-start(f32[128,512]{1,0:T(8,128)S(1)} %broadcast_select_fusion.3), channel_id=1, source_target_pairs={{228,100},{236,108},{244,116},{252,124},{229,101},{237,109},{245,1... | collective-permute-start | bytes 786440 | tf_op jit(solution)/shard_map/ppermute | solution.py:54
  16.2 9.0 %collective-permute-start.5 = (f32[128,512]{1,0:T(8,128)S(1)}, f32[128,512]{1,0:T(8,128)}, u32[]{:S(2)}, u32[]{:S(2)}) collective-permute-start(f32[128,512]{1,0:T(8,128)S(1)} %broadcast_select_fusion.3), channel_id=1, source_target_pairs={{228,68},{236,76},{244,84},{252,92},{224,128},{232,136},{240,144},... | collective-permute-start | bytes 786440 | tf_op jit(solution)/shard_map/ppermute | solution.py:54
  17.5 8.4 %collective-permute-start.6 = (f32[128,512]{1,0:T(8,128)S(1)}, f32[128,512]{1,0:T(8,128)}, u32[]{:S(2)}, u32[]{:S(2)}) collective-permute-start(f32[128,512]{1,0:T(8,128)S(1)} %broadcast_select_fusion.3), channel_id=1, source_target_pairs={{228,36},{236,44},{244,52},{252,60},{224,160},{232,168},{240,176},... | collective-permute-start | bytes 786440 | tf_op jit(solution)/shard_map/ppermute | solution.py:54
  18.9 17.0 %collective-permute-start.7 = (f32[128,512]{1,0:T(8,128)S(1)}, f32[128,512]{1,0:T(8,128)}, u32[]{:S(2)}, u32[]{:S(2)}) collective-permute-start(f32[128,512]{1,0:T(8,128)S(1)} %broadcast_select_fusion.3), channel_id=1, source_target_pairs={{228,4},{236,12},{244,20},{252,28},{224,192},{232,200},{240,208},{... | collective-permute-start | bytes 786440 | tf_op jit(solution)/shard_map/ppermute | solution.py:54
  21.3 1.0 copy-start.1
  23.1 22.1 %collective-permute-start.12 = (f32[128,512]{1,0:T(8,128)}, f32[128,512]{1,0:T(8,128)}, u32[]{:S(2)}, u32[]{:S(2)}) collective-permute-start(f32[128,512]{1,0:T(8,128)} %get-tuple-element.7), channel_id=1, source_target_pairs={{252,228},{253,229},{254,230},{255,231}} | collective-permute-start | bytes 786440 | tf_op jit(solution)/shard_map/ppermute | solution.py:54
  24.5 25.7 %collective-permute-start.13 = (f32[128,512]{1,0:T(8,128)}, f32[128,512]{1,0:T(8,128)S(1)}, u32[]{:S(2)}, u32[]{:S(2)}) collective-permute-start(f32[128,512]{1,0:T(8,128)} %get-tuple-element.5), channel_id=1, source_target_pairs={{252,236},{253,237},{254,238},{255,239}} | collective-permute-start | bytes 786440 | tf_op jit(solution)/shard_map/ppermute | solution.py:54
  25.2 25.1 %collective-permute-start.14 = (f32[128,512]{1,0:T(8,128)}, f32[128,512]{1,0:T(8,128)S(1)}, u32[]{:S(2)}, u32[]{:S(2)}) collective-permute-start(f32[128,512]{1,0:T(8,128)} %get-tuple-element.6), channel_id=1, source_target_pairs={{252,244},{253,245},{254,246},{255,247}} | collective-permute-start | bytes 786440 | tf_op jit(solution)/shard_map/ppermute | solution.py:54
  37.3 14.3 %collective-permute-start.10 = (f32[128,512]{1,0:T(8,128)S(1)}, f32[128,512]{1,0:T(8,128)S(1)}, u32[]{:S(2)}, u32[]{:S(2)}) collective-permute-start(f32[128,512]{1,0:T(8,128)S(1)} %add_select_fusion.1), channel_id=1, source_target_pairs={{4,12},{12,20},{20,28},{28,4},{36,44},{44,52},{52,60},{60,36},{68,... | collective-permute-start | bytes 786440 | tf_op jit(solution)/shard_map/ppermute | solution.py:54
  41.6 10.0 %collective-permute-start.8 = (f32[128,512]{1,0:T(8,128)S(1)}, f32[128,512]{1,0:T(8,128)S(1)}, u32[]{:S(2)}, u32[]{:S(2)}) collective-permute-start(f32[128,512]{1,0:T(8,128)S(1)} %add_select_fusion.1), channel_id=1, source_target_pairs={{4,28},{12,4},{20,12},{28,20},{36,60},{44,36},{52,44},{60,52},{68,... | collective-permute-start | bytes 786440 | tf_op jit(solution)/shard_map/ppermute | solution.py:54
  45.3 8.7 %collective-permute-start.9 = (f32[128,512]{1,0:T(8,128)S(1)}, f32[128,512]{1,0:T(8,128)S(1)}, u32[]{:S(2)}, u32[]{:S(2)}) collective-permute-start(f32[128,512]{1,0:T(8,128)S(1)} %add_select_fusion.1), channel_id=1, source_target_pairs={{4,20},{12,28},{20,4},{28,12},{36,52},{44,60},{52,36},{60,44},{68,... | collective-permute-start | bytes 786440 | tf_op jit(solution)/shard_map/ppermute | solution.py:54
  51.4 3.6 %collective-permute-start.15 = (f32[128,512]{1,0:T(8,128)S(1)}, f32[128,512]{1,0:T(8,128)S(1)}, u32[]{:S(2)}, u32[]{:S(2)}) collective-permute-start(f32[128,512]{1,0:T(8,128)S(1)} %slice_select_fusion), channel_id=1, source_target_pairs={{0,4},{4,0},{8,12},{12,8},{16,20},{20,16},{24,28},{28,24},{32,36},... | collective-permute-start | bytes 786440 | tf_op jit(solution)/shard_map/ppermute | solution.py:54
  51.5 20.4 %copy-start.7 = (f32[128,512]{1,0:T(8,128)}, f32[128,512]{1,0:T(8,128)S(1)}, u32[]{:S(2)}) copy-start(f32[128,512]{1,0:T(8,128)S(1)} %collective-permute-done.10) | copy-start | bytes 786436
  51.6 20.4 %copy-start.8 = (f32[128,512]{1,0:T(8,128)}, f32[128,512]{1,0:T(8,128)S(1)}, u32[]{:S(2)}) copy-start(f32[128,512]{1,0:T(8,128)S(1)} %collective-permute-done.8) | copy-start | bytes 786436
  54.0 18.0 %copy-start.9 = (f32[128,512]{1,0:T(8,128)}, f32[128,512]{1,0:T(8,128)S(1)}, u32[]{:S(2)}) copy-start(f32[128,512]{1,0:T(8,128)S(1)} %collective-permute-done.9) | copy-start | bytes 786436
  55.1 34.4 %collective-permute-start.11 = (f32[512,512]{1,0:T(8,128)}, f32[512,512]{1,0:T(8,128)}, u32[]{:S(2)}, u32[]{:S(2)}) collective-permute-start(f32[512,512]{1,0:T(8,128)} %pad_maximum_fusion), channel_id=1, source_target_pairs={{0,4},{4,0},{8,12},{12,8},{16,20},{20,16},{24,28},{28,24},{32,36},... | collective-permute-start | bytes 3145736 | tf_op jit(solution)/shard_map/ppermute | solution.py:54
  55.1 3.4 %collective-permute-start.16 = (f32[128,512]{1,0:T(8,128)S(1)}, f32[128,512]{1,0:T(8,128)S(1)}, u32[]{:S(2)}, u32[]{:S(2)}) collective-permute-start(f32[128,512]{1,0:T(8,128)S(1)} %broadcast_select_fusion.2), channel_id=1, source_target_pairs={{228,100},{236,108},{244,116},{252,124},{229,101},{237,109},{245,1... | collective-permute-start | bytes 786440 | tf_op jit(solution)/shard_map/ppermute | solution.py:54
  55.8 2.7 %collective-permute-start.17 = (f32[128,512]{1,0:T(8,128)S(1)}, f32[128,512]{1,0:T(8,128)S(1)}, u32[]{:S(2)}, u32[]{:S(2)}) collective-permute-start(f32[128,512]{1,0:T(8,128)S(1)} %broadcast_select_fusion.2), channel_id=1, source_target_pairs={{228,68},{236,76},{244,84},{252,92},{224,128},{232,136},{240,144},... | collective-permute-start | bytes 786440 | tf_op jit(solution)/shard_map/ppermute | solution.py:54
  56.5 2.0 %collective-permute-start.18 = (f32[128,512]{1,0:T(8,128)S(1)}, f32[128,512]{1,0:T(8,128)S(1)}, u32[]{:S(2)}, u32[]{:S(2)}) collective-permute-start(f32[128,512]{1,0:T(8,128)S(1)} %broadcast_select_fusion.2), channel_id=1, source_target_pairs={{228,36},{236,44},{244,52},{252,60},{224,160},{232,168},{240,176},... | collective-permute-start | bytes 786440 | tf_op jit(solution)/shard_map/ppermute | solution.py:54
  57.2 14.0 %collective-permute-start.19 = (f32[128,512]{1,0:T(8,128)S(1)}, f32[128,512]{1,0:T(8,128)S(1)}, u32[]{:S(2)}, u32[]{:S(2)}) collective-permute-start(f32[128,512]{1,0:T(8,128)S(1)} %broadcast_select_fusion.2), channel_id=1, source_target_pairs={{228,4},{236,12},{244,20},{252,28},{224,192},{232,200},{240,208},{... | collective-permute-start | bytes 786440 | tf_op jit(solution)/shard_map/ppermute | solution.py:54
  72.0 7.8 %collective-permute-start.20 = (f32[128,512]{1,0:T(8,128)}, f32[128,512]{1,0:T(8,128)}, u32[]{:S(2)}, u32[]{:S(2)}) collective-permute-start(f32[128,512]{1,0:T(8,128)} %add_select_fusion), channel_id=1, source_target_pairs={{4,28},{12,4},{20,12},{28,20},{36,60},{44,36},{52,44},{60,52},{68,... | collective-permute-start | bytes 786440 | tf_op jit(solution)/shard_map/ppermute | solution.py:54
  75.3 9.0 %collective-permute-start.21 = (f32[128,512]{1,0:T(8,128)}, f32[128,512]{1,0:T(8,128)}, u32[]{:S(2)}, u32[]{:S(2)}) collective-permute-start(f32[128,512]{1,0:T(8,128)} %add_select_fusion), channel_id=1, source_target_pairs={{4,20},{12,28},{20,4},{28,12},{36,52},{44,60},{52,36},{60,44},{68,... | collective-permute-start | bytes 786440 | tf_op jit(solution)/shard_map/ppermute | solution.py:54
  77.5 9.6 %collective-permute-start.22 = (f32[128,512]{1,0:T(8,128)}, f32[128,512]{1,0:T(8,128)}, u32[]{:S(2)}, u32[]{:S(2)}) collective-permute-start(f32[128,512]{1,0:T(8,128)} %add_select_fusion), channel_id=1, source_target_pairs={{4,12},{12,20},{20,28},{28,4},{36,44},{44,52},{52,60},{60,36},{68,... | collective-permute-start | bytes 786440 | tf_op jit(solution)/shard_map/ppermute | solution.py:54
  89.3 4.3 %collective-permute-start.23 = (f32[512,512]{1,0:T(8,128)}, f32[512,512]{1,0:T(8,128)}, u32[]{:S(2)}, u32[]{:S(2)}) collective-permute-start(f32[512,512]{1,0:T(8,128)} %pad_maximum_fusion.1), channel_id=1, source_target_pairs={{0,4},{4,0},{8,12},{12,8},{16,20},{20,16},{24,28},{28,24},{32,36},... | collective-permute-start | bytes 3145736 | tf_op jit(solution)/shard_map/ppermute | solution.py:54
  95.4 7.6 %copy-start.4 = (f32[1024,1024]{1,0:T(8,128)S(1)}, f32[1024,1024]{1,0:T(8,128)}, u32[]{:S(2)}) copy-start(f32[1024,1024]{1,0:T(8,128)} %param.6) | copy-start | bytes 12582916
  97.8 7.2 %copy-start.2 = (f32[512,512]{1,0:T(8,128)S(1)}, f32[512,512]{1,0:T(8,128)}, u32[]{:S(2)}) copy-start(f32[512,512]{1,0:T(8,128)} %copy-done.1) | copy-start | bytes 3145732
  97.8 7.2 %copy-start.3 = (f32[1024,512]{1,0:T(8,128)S(1)}, f32[1024,512]{1,0:T(8,128)}, u32[]{:S(2)}) copy-start(f32[1024,512]{1,0:T(8,128)} %param.4) | copy-start | bytes 6291460
  97.8 12.9 %collective-permute-start.28 = (f32[128,1024]{1,0:T(8,128)S(1)}, f32[128,1024]{1,0:T(8,128)S(1)}, u32[]{:S(2)}, u32[]{:S(2)}) collective-permute-start(f32[128,1024]{1,0:T(8,128)S(1)} %fusion.28), channel_id=1, source_target_pairs={{0,3},{1,0},{2,1},{3,2},{4,7},{5,4},{6,5},{7,6},{8,11},{9,8},{10,9... | collective-permute-start | bytes 1572872 | tf_op jit(solution)/shard_map/ppermute | solution.py:79
  100.4 14.8 %collective-permute-start.29 = (f32[128,1024]{1,0:T(8,128)S(1)}, f32[128,1024]{1,0:T(8,128)S(1)}, u32[]{:S(2)}, u32[]{:S(2)}) collective-permute-start(f32[128,1024]{1,0:T(8,128)S(1)} %fusion.24), channel_id=1, source_target_pairs={{0,1},{1,2},{2,3},{3,0},{4,5},{5,6},{6,7},{7,4},{8,9},{9,10},{10,1... | collective-permute-start | bytes 1572872 | tf_op jit(solution)/shard_map/ppermute | solution.py:78
  100.4 21.4 %collective-permute-start.24 = (f32[128,1024]{1,0:T(8,128)S(1)}, f32[128,1024]{1,0:T(8,128)S(1)}, u32[]{:S(2)}, u32[]{:S(2)}) collective-permute-start(f32[128,1024]{1,0:T(8,128)S(1)} %fusion.38), channel_id=1, source_target_pairs={{0,3},{1,0},{2,1},{3,2},{4,7},{5,4},{6,5},{7,6},{8,11},{9,8},{10,9... | collective-permute-start | bytes 1572872 | tf_op jit(solution)/shard_map/ppermute | solution.py:79
  103.0 23.3 %collective-permute-start.25 = (f32[128,1024]{1,0:T(8,128)S(1)}, f32[128,1024]{1,0:T(8,128)S(1)}, u32[]{:S(2)}, u32[]{:S(2)}) collective-permute-start(f32[128,1024]{1,0:T(8,128)S(1)} %fusion.34), channel_id=1, source_target_pairs={{0,1},{1,2},{2,3},{3,0},{4,5},{5,6},{6,7},{7,4},{8,9},{9,10},{10,1... | collective-permute-start | bytes 1572872 | tf_op jit(solution)/shard_map/ppermute | solution.py:78
  111.8 15.8 %collective-permute-start.31 = (f32[64,1024]{1,0:T(8,128)S(1)}, f32[64,1024]{1,0:T(8,128)S(1)}, u32[]{:S(2)}, u32[]{:S(2)}) collective-permute-start(f32[64,1024]{1,0:T(8,128)S(1)} %slice_add_fusion), channel_id=1, source_target_pairs={{0,3},{1,0},{2,1},{3,2},{4,7},{5,4},{6,5},{7,6},{8,11},{9,8},{10,9... | collective-permute-start | bytes 786440 | tf_op jit(solution)/shard_map/ppermute | solution.py:84
  116.2 14.3 %collective-permute-start.30 = (f32[64,1024]{1,0:T(8,128)S(1)}, f32[64,1024]{1,0:T(8,128)S(1)}, u32[]{:S(2)}, u32[]{:S(2)}) collective-permute-start(f32[64,1024]{1,0:T(8,128)S(1)} %slice_add_fusion.2), channel_id=1, source_target_pairs={{0,1},{1,2},{2,3},{3,0},{4,5},{5,6},{6,7},{7,4},{8,9},{9,10},{10,1... | collective-permute-start | bytes 786440 | tf_op jit(solution)/shard_map/ppermute | solution.py:83
  122.9 9.9 %collective-permute-start.27 = (f32[64,1024]{1,0:T(8,128)S(1)}, f32[64,1024]{1,0:T(8,128)S(1)}, u32[]{:S(2)}, u32[]{:S(2)}) collective-permute-start(f32[64,1024]{1,0:T(8,128)S(1)} %slice_add_fusion.4), channel_id=1, source_target_pairs={{0,3},{1,0},{2,1},{3,2},{4,7},{5,4},{6,5},{7,6},{8,11},{9,8},{10,9... | collective-permute-start | bytes 786440 | tf_op jit(solution)/shard_map/ppermute | solution.py:84
  127.5 7.4 %collective-permute-start.26 = (f32[64,1024]{1,0:T(8,128)S(1)}, f32[64,1024]{1,0:T(8,128)S(1)}, u32[]{:S(2)}, u32[]{:S(2)}) collective-permute-start(f32[64,1024]{1,0:T(8,128)S(1)} %slice_add_fusion.6), channel_id=1, source_target_pairs={{0,1},{1,2},{2,3},{3,0},{4,5},{5,6},{6,7},{7,4},{8,9},{9,10},{10,1... | collective-permute-start | bytes 786440 | tf_op jit(solution)/shard_map/ppermute | solution.py:83

commit v2 on v0

v2 whole, which is shorter than its diff:
```python
import jax
import jax.numpy as jnp
from jax import lax
from jax.experimental import pallas as pl
from jax.experimental.pallas import tpu as pltpu
from jax.sharding import PartitionSpec as P

STEPS = 2
LEAD = (((0,), (0,)), ((), ()))
LAST = (((1,), (1,)), ((), ()))
NZ, NY, NX = 8, 4, 4
CHIPS = NZ * NY
ROOT = 2 * CHIPS - 1
VMEM_LIMIT = 48 * 1024 * 1024


def rank(z, y, c):
    return (z * NY + y) * 2 + c


SWAP = [(r, r ^ 1) for r in range(2 * CHIPS)]
ALONG_Y = [[rank(z, y, c) for y in range(NY)] for z in range(NZ) for c in range(2)]
ALONG_Z = [[rank(z, y, c) for z in range(NZ)] for y in range(NY) for c in range(2)]
X_RIGHT = [(q, (q + 1) % NX) for q in range(NX)]
X_LEFT = [(q, (q - 1) % NX) for q in range(NX)]


def split(x):
    high = x.astype(jnp.bfloat16)
    return high, (x - high.astype(jnp.float32)).astype(jnp.bfloat16)


def dot3(a, b, dims):
    def one(x, y):
        return lax.dot_general(x, y, dims, preferred_element_type=jnp.float32)

    return one(a[0], b[0]) + (one(a[0], b[1]) + one(a[1], b[0]))


def solve_kernel(cot_ref, panel_ref, dinv_ref, *out_refs):
    bs = dinv_ref.shape[1]
    half = bs // 8

    def put(k, solved):
        for quarter in range(4):
            for h in range(2):
                row = (quarter * 2 + h) * half
                out_refs[h][quarter, k] = solved[row : row + half]

    solved1 = dot3(split(dinv_ref[1]), split(cot_ref[bs:]), LEAD)
    put(1, solved1)
    left = cot_ref[:bs] - dot3(split(panel_ref[...]), split(solved1), LEAD)
    put(0, dot3(split(dinv_ref[0]), split(left), LEAD))


def solve(cotangent, panel, dinv):
    steps, bs, _ = dinv.shape
    rows, cols = cotangent.shape
    return pl.pallas_call(
        solve_kernel,
        grid=(1,),
        in_specs=[
            pl.BlockSpec((rows, cols), lambda i: (0, 0)),
            pl.BlockSpec((bs, bs), lambda i: (1, 0)),
            pl.BlockSpec((steps, bs, bs), lambda i: (0, 0, 0)),
        ],
        out_specs=[pl.BlockSpec((4, steps, bs // 8, cols), lambda i: (0, 0, 0, 0))] * 2,
        out_shape=[jax.ShapeDtypeStruct((4, steps, bs // 8, cols), jnp.float32)] * 2,
        compiler_params=pltpu.CompilerParams(vmem_limit_bytes=VMEM_LIMIT),
        cost_estimate=pl.CostEstimate(flops=18 * bs * bs * cols, bytes_accessed=7 << 20, transcendentals=0),
    )(cotangent, panel, dinv)


def update_kernel(at_ref, cot_ref, panel_ref, mine_ref, other_ref, out_ref, whole, high, low):
    i = pl.program_id(0)
    half = mine_ref.shape[2]
    tile = out_ref.shape[0]
    core = at_ref[2]

    @pl.when(i == 0)
    def _():
        for k in range(STEPS):
            for quarter in range(4):
                a, b = mine_ref[quarter, k], other_ref[quarter, k]
                for h in range(2):
                    rows = jnp.where(core == h, a, b)
                    at = pl.ds(((k * 4 + quarter) * 2 + h) * half, half)
                    whole[at, :] = rows
                    high[at, :], low[at, :] = split(rows)

    @pl.when(at_ref[0] != ROOT)
    def _():
        product = dot3(split(panel_ref[...]), (high[...], low[...]), LEAD)
        out_ref[...] = cot_ref[...] - product

    @pl.when(at_ref[0] == ROOT)
    def _():
        out_ref[...] = whole[pl.ds(pl.multiple_of(i * tile, tile), tile), :]


def update(at, cotangent, panel, mine, other):
    rows, cols = cotangent.shape
    tile = rows // 4
    halves = pl.BlockSpec(mine.shape, lambda i, at: (0, 0, 0, 0))
    return pl.pallas_call(
        update_kernel,
        grid_spec=pltpu.PrefetchScalarGridSpec(
            num_scalar_prefetch=1,
            grid=(4,),
            in_specs=[
                pl.BlockSpec((tile, cols), lambda i, at: (i, 0)),
                pl.BlockSpec((rows, tile), lambda i, at: (0, i)),
                halves,
                halves,
            ],
            out_specs=pl.BlockSpec((tile, cols), lambda i, at: (i, 0)),
            scratch_shapes=[
                pltpu.VMEM((rows, cols), jnp.float32),
                pltpu.VMEM((rows, cols), jnp.bfloat16),
                pltpu.VMEM((rows, cols), jnp.bfloat16),
            ],
        ),
        out_shape=jax.ShapeDtypeStruct((rows, cols), jnp.float32),
        compiler_params=pltpu.CompilerParams(vmem_limit_bytes=VMEM_LIMIT),
        cost_estimate=pl.CostEstimate(flops=6 * rows * rows * cols, bytes_accessed=10 << 20, transcendentals=0),
    )(at, cotangent, panel, mine, other)


def grad_kernel(at_ref, mine_ref, other_ref, own_ref, left_ref, right_ref, upper_ref, lower_ref, out_ref, high, low):
    i = pl.program_id(0)
    me, q, core = at_ref[0], at_ref[1], at_ref[2]
    half = mine_ref.shape[2]
    quarter = 2 * half
    tile = out_ref.shape[2]
    local_rows = 4 * tile

    @pl.when(i == 0)
    def _():
        for j in range(4):
            for k in range(STEPS):
                a, b = mine_ref[j, k], other_ref[j, k]
                for h in range(2):
                    at = pl.ds((k * 2 + h) * half, half)
                    high[j, at, :], low[j, at, :] = split(-jnp.where(core == h, a, b))

    def term(away, saved):
        j = lax.rem(q + away, NX)
        return dot3((high[j], low[j]), split(saved), LAST)

    total = term(0, own_ref[...]) + term(3, left_ref[...]) + term(1, right_ref[...])
    total += term(2, jnp.where(i < 2, upper_ref[...], lower_ref[...]))
    column = me * local_rows + i * tile + lax.broadcasted_iota(jnp.int32, (quarter, tile), 1)
    row = lax.broadcasted_iota(jnp.int32, (quarter, tile), 0) + q * quarter
    for k in range(STEPS):
        limit = row + (2 * CHIPS * local_rows - (STEPS - k) * 4 * quarter)
        part = total[k * quarter : (k + 1) * quarter]
        out_ref[k] = jnp.where(column <= limit, part, jnp.float32(0.0))


def grad(at, mine, other, own, left, right, upper, lower):
    _, _, half, cols = mine.shape
    rows = own.shape[0]
    tile = rows // 4
    halves = pl.BlockSpec(mine.shape, lambda i, at: (0, 0, 0, 0))
    tiled = pl.BlockSpec((tile, cols), lambda i, at: (i, 0))
    first = pl.BlockSpec((tile, cols), lambda i, at: (jnp.minimum(i, 1), 0))
    last = pl.BlockSpec((tile, cols), lambda i, at: (jnp.maximum(i - 2, 0), 0))
    return pl.pallas_call(
        grad_kernel,
        grid_spec=pltpu.PrefetchScalarGridSpec(
            num_scalar_prefetch=1,
            grid=(4,),
            in_specs=[halves, halves, tiled, tiled, tiled, first, last],
            out_specs=pl.BlockSpec((STEPS, 2 * half, tile), lambda i, at: (0, 0, i)),
            scratch_shapes=[
                pltpu.VMEM((4, STEPS * 2 * half, cols), jnp.bfloat16),
                pltpu.VMEM((4, STEPS * 2 * half, cols), jnp.bfloat16),
            ],
        ),
        out_shape=jax.ShapeDtypeStruct((STEPS, 2 * half, rows), jnp.float32),
        compiler_params=pltpu.CompilerParams(vmem_limit_bytes=VMEM_LIMIT),
        cost_estimate=pl.CostEstimate(flops=96 * half * rows * cols, bytes_accessed=12 << 20, transcendentals=0),
    )(at, mine, other, own, left, right, upper, lower)


def on_device(cotangent, saved, panel, dinv):
    bs = dinv.shape[1]
    local_rows, cols = cotangent.shape
    half = bs // 8
    me = lax.axis_index("rows")
    q = lax.axis_index("cols")
    c = me % 2
    at = jnp.stack([me, q, c]).astype(jnp.int32)

    def swap(x):
        return lax.ppermute(x, "rows", SWAP)

    def right(x):
        return lax.ppermute(x, "cols", X_RIGHT)

    def left(x):
        return lax.ppermute(x, "cols", X_LEFT)

    def scatter(x, groups):
        count = len(groups[0])
        blocks = x.reshape(count, -1, cols)
        return lax.all_to_all(blocks, "rows", 0, 0, axis_index_groups=groups)[count - 1]

    def gather(x, groups):
        count = len(groups[0])
        blocks = jnp.broadcast_to(x[None], (count,) + x.shape)
        return lax.all_to_all(blocks, "rows", 0, 0, axis_index_groups=groups).reshape(-1, cols)

    from_left, from_right = right(saved), left(saved)

    given, kept = solve(cotangent, panel, dinv)
    mine = jnp.where(c == 1, kept.reshape(bs, cols), swap(given.reshape(bs, cols)))
    mine = scatter(scatter(mine, ALONG_Y), ALONG_Z)
    mine = gather(mine, ALONG_Z)
    upper, lower = from_left[: local_rows // 2], from_right[local_rows // 2 :]
    mine, upper, lower = lax.optimization_barrier((mine, upper, lower))
    upper, lower = right(upper), left(lower)
    mine = gather(mine, ALONG_Y)
    mine, other, upper, lower = lax.optimization_barrier((mine, swap(mine), upper, lower))

    wide = lax.all_to_all(mine.reshape(4, STEPS * half, cols), "cols", 0, 0)
    shape = (4, STEPS, half, cols)
    carried = update(at, cotangent, panel, mine.reshape(shape), other.reshape(shape))
    wide, carried = lax.optimization_barrier((wide, carried))
    other = swap(wide.reshape(4 * STEPS * half, cols))
    factor = grad(at, wide.reshape(shape), other.reshape(shape), saved, from_left, from_right, upper, lower)
    return carried, factor


def solution(mesh):
    return jax.shard_map(
        on_device,
        mesh=mesh,
        in_specs=(P("rows", "cols"), P("rows", "cols"), P(None, "rows"), P()),
        out_specs=(P("rows", "cols"), P(None, "cols", "rows")),
        check_vma=False,
    )
```

time: 476 us -> 128 us (0.27)
  waiting for transfers between devices: 414 us -> 32.9 us
  blocking collectives: 0 us -> 33.7 us
  matrix products: 30.3 us -> 0 us
  starting transfers between devices: 0.34 us -> 26.1 us
  Pallas kernels: 0 us -> 20.7 us
  between operations: 13.9 us -> 0.71 us
  other arithmetic: 5.86 us -> 0.31 us
    psum x2 -> x0, waiting for transfers between devices: 366 us -> none  [on_device(): block_rows = lax.psum(owned_rows, 'rows')]
    reduce_scatter x2 -> x0, waiting for transfers between devices: 48.6 us -> none  [on_device(): lax.psum_scatter(grad_rows(jnp.int32(0), lax.axis_size('cols') * (BS // l...]
    all_to_all x0 -> x2, blocking collectives: none -> 33.7 us  [scatter(): lax.all_to_all(blocks, 'rows', 0, 0, axis_index_groups=groups)[count - 1]]
    dot_general x6 -> x0, matrix products: 30.3 us -> none  [the longest x2 13.7 us: on_device(): lax.dot_general(panel[k * BS:(k + 1) * BS], solved, contract_lead, precis...]
    pallas_call x0 -> x3, Pallas kernels: none -> 20.7 us  [the longest x1 7.98 us: grad(): pl.pallas_call(grad_kernel, grid_spec=pltpu.PrefetchScalarGridSpec(num_sc...]
    ppermute x0 -> x7, waiting for transfers between devices: none -> 18.8 us  [the longest x2 16.5 us: right(): return lax.ppermute(x, 'cols', X_RIGHT)]
    ppermute x0 -> x7, starting transfers between devices: none -> 14.8 us  [the longest x3 9.31 us: swap(): return lax.ppermute(x, 'rows', SWAP)]
    all_to_all x0 -> x3, waiting for transfers between devices: none -> 14.1 us  [the longest x2 11 us: gather(): lax.all_to_all(blocks, 'rows', 0, 0, axis_index_groups=groups)]
  transfers between devices with their start and end apart: 4 -> 10, of which waited for: 4 -> 5; matrix products, arithmetic and copies ran while one was open for 6% -> 4% of each run, Pallas kernels for 0% -> 6%
where the time goes in v2:
time: 128 us; the launch traced here: 127 us
  blocking collectives  33.7 us (26%)
  waiting for transfers between devices  32.9 us (26%)
  starting transfers between devices  26.1 us (20%)
  Pallas kernels  20.7 us (16%)
  local copies, waits for them, and re-layouts  12.4 us (10%)
    all_to_all x2, blocking collectives, scatter(): lax.all_to_all(blocks, 'rows', 0, 0, axis_index_groups=groups)[count - 1]  33.7 us
    ppermute x2, waiting for transfers between devices, right(): return lax.ppermute(x, 'cols', X_RIGHT)  16.5 us
    all_to_all x2, waiting for transfers between devices, gather(): lax.all_to_all(blocks, 'rows', 0, 0, axis_index_groups=groups)  11 us
    ppermute x3, starting transfers between devices, swap(): return lax.ppermute(x, 'rows', SWAP)  9.31 us
    pallas_call x1, Pallas kernels, grad(): pl.pallas_call(grad_kernel, grid_spec=pltpu.PrefetchScalarGridSpec(num_sc...  7.98 us
    pallas_call x1, Pallas kernels, update(): pl.pallas_call(update_kernel, grid_spec=pltpu.PrefetchScalarGridSpec(num_...  7.97 us
    all_to_all x2, starting transfers between devices, gather(): lax.all_to_all(blocks, 'rows', 0, 0, axis_index_groups=groups)  7.82 us
    unnamed x12, local copies, waits for them, and re-layouts  5.99 us
  transfers between devices with their start and end apart: 10, of which 5 were waited for; matrix products, arithmetic and copies ran while one was open for 4% of the time, Pallas kernels for 6%

profile of v2, /device:TPU:1, one launch (start us, length us, event | category | flops | bytes accessed | tf_op | source)
XLA Modules:
  0.0 126.9 jit_solution(4323227388834059470)
XLA Ops:
  0.6 0.0 copy-start
  0.6 1.6 %copy-done = f32[1024,512]{1,0:T(8,128)S(1)} copy-done((f32[1024,512]{1,0:T(8,128)S(1)}, f32[1024,512]{1,0:T(8,128)}, u32[]{:S(2)}) %copy-start) | copy-done | bytes 2097176
  2.2 4.8 %shard_map.59 = (f32[4,2,64,512]{3,2,1,0:T(8,128)S(1)}, f32[4,2,64,512]{3,2,1,0:T(8,128)S(1)}) custom-call(f32[1024,512]{1,0:T(8,128)S(1)} %copy-done, f32[1024,1024]{1,0:T(8,128)} %panel_ref.3, f32[2,512,512]{2,1,0:T(8,128)} %dinv_ref.1), custom_call_target="tpu_custom_call" | custom-call | flops 2415919104 | bytes 7340032 | tf_op jit(solution)/shard_map/pallas_call | solution.py:59
  7.0 3.3 %collective-permute-start = (f32[512,512]{1,0:T(8,128)S(1)}, f32[512,512]{1,0:T(8,128)S(1)}, u32[]{:S(2)}, u32[]{:S(2)}) collective-permute-start(f32[512,512]{1,0:T(8,128)S(1)} %bitcast.20), channel_id=1, source_target_pairs={{0,4},{4,0},{8,12},{12,8},{16,20},{20,16},{24,28},{28,24},{32,36},... | collective-permute-start | bytes 3145736 | tf_op jit(solution)/shard_map/ppermute | solution.py:196
  10.3 0.0 collective-permute-start.1
  10.3 2.7 %collective-permute-start.2 = (f32[1024,512]{1,0:T(8,128)}, f32[1024,512]{1,0:T(8,128)}, u32[]{:S(2)}, u32[]{:S(2)}) collective-permute-start(f32[1024,512]{1,0:T(8,128)} %own_ref.1), channel_id=1, source_target_pairs={{0,3},{1,0},{2,1},{3,2},{4,7},{5,4},{6,5},{7,6},{8,11},{9,8},{10,9... | collective-permute-start | bytes 6291464 | tf_op jit(solution)/shard_map/ppermute | solution.py:202
  13.0 0.0 collective-permute-done
  13.0 0.2 bitcast_select_fusion
  13.3 16.6 %all_to_all.25 = f32[4,128,512]{2,1,0:T(8,128)S(1)} all-to-all(f32[4,128,512]{2,1,0:T(8,128)S(1)} %bitcast.23), channel_id=1, replica_groups={{0,8,16,24},{4,12,20,28},{32,40,48,56},{36,44,52,60},{64,72,80,88},{68,..., dimensions={0} | all-to-all | bytes 2097152 | tf_op jit(solution)/shard_map/all_to_all | solution.py:207
  29.8 17.1 %all_to_all.26 = f32[8,16,512]{2,1,0:T(8,128)S(1)} all-to-all(f32[8,16,512]{2,1,0:T(8,128)S(1)} %bitcast.25), channel_id=1, replica_groups={{0,32,64,96,128,160,192,224},{4,36,68,100,132,164,196,228},{8,40,72,104..., dimensions={0} | all-to-all | bytes 524288 | tf_op jit(solution)/shard_map/all_to_all | solution.py:207
  47.0 0.7 broadcast_in_dim.14
  47.7 3.4 %all-to-all-start.2 = ((f32[8,16,512]{2,1,0:T(8,128)}), f32[8,16,512]{2,1,0:T(8,128)S(1)}, u32[]{:S(2)}, u32[]{:S(2)}) async-start(f32[8,16,512]{2,1,0:T(8,128)} %broadcast_in_dim.14), calls=%async_computation.2 | async-start | bytes 524288 | tf_op jit(solution)/shard_map/all_to_all | solution.py:212
  51.1 7.9 %collective-permute-done.1.left_ref = f32[1024,512]{1,0:T(8,128)} collective-permute-done((f32[1024,512]{1,0:T(8,128)}, f32[1024,512]{1,0:T(8,128)}, u32[]{:S(2)}, u32[]{:S(2)}) %collective-permute-start.1) | collective-permute-done | bytes 2097184 | tf_op jit(solution)/shard_map/ppermute | solution.py:199
  59.1 2.3 %slice.18 = f32[512,512]{1,0:T(8,128)} slice(f32[1024,512]{1,0:T(8,128)} %collective-permute-done.1.left_ref), slice={[0:512], [0:512]} | slice | bytes 2097152 | tf_op jit(solution)/shard_map/slice | solution.py:220
  61.3 0.0 collective-permute-done.2.right_ref
  61.3 2.3 %slice.19 = f32[512,512]{1,0:T(8,128)} slice(f32[1024,512]{1,0:T(8,128)} %collective-permute-done.2.right_ref), slice={[512:1024], [0:512]} | slice | bytes 2097152 | tf_op jit(solution)/shard_map/slice | solution.py:220
  63.7 0.0 all-to-all-done.2
  63.7 1.1 broadcast_in_dim.15
  64.8 0.0 copy-start.1
  64.8 4.4 %all-to-all-start.3 = ((f32[4,128,512]{2,1,0:T(8,128)}), f32[4,128,512]{2,1,0:T(8,128)}, u32[]{:S(2)}, u32[]{:S(2)}) async-start(f32[4,128,512]{2,1,0:T(8,128)} %broadcast_in_dim.15), calls=%async_computation.3 | async-start | bytes 2097152 | tf_op jit(solution)/shard_map/all_to_all | solution.py:212
  69.2 0.1 collective-permute-start.4
  69.3 2.7 %collective-permute-start.5 = (f32[512,512]{1,0:T(8,128)}, f32[512,512]{1,0:T(8,128)}, u32[]{:S(2)}, u32[]{:S(2)}) collective-permute-start(f32[512,512]{1,0:T(8,128)} %slice.19), channel_id=1, source_target_pairs={{0,3},{1,0},{2,1},{3,2},{4,7},{5,4},{6,5},{7,6},{8,11},{9,8},{10,9... | collective-permute-start | bytes 3145736 | tf_op jit(solution)/shard_map/ppermute | solution.py:202
  71.9 11.0 %all-to-all-done.3 = f32[4,128,512]{2,1,0:T(8,128)} async-done(((f32[4,128,512]{2,1,0:T(8,128)}), f32[4,128,512]{2,1,0:T(8,128)}, u32[]{:S(2)}, u32[]{:S(2)}) %all-to-all-start.3) | async-done | bytes 1048608 | tf_op jit(solution)/shard_map/all_to_all | solution.py:212
  82.9 2.4 %collective-permute-start.3 = (f32[512,512]{1,0:T(8,128)}, f32[512,512]{1,0:T(8,128)S(1)}, u32[]{:S(2)}, u32[]{:S(2)}) collective-permute-start(f32[512,512]{1,0:T(8,128)} %bitcast.6), channel_id=1, source_target_pairs={{0,4},{4,0},{8,12},{12,8},{16,20},{20,16},{24,28},{28,24},{32,36},... | collective-permute-start | bytes 3145736 | tf_op jit(solution)/shard_map/ppermute | solution.py:196
  85.3 8.6 %collective-permute-done.4.upper_ref = f32[512,512]{1,0:T(8,128)S(1)} collective-permute-done((f32[512,512]{1,0:T(8,128)}, f32[512,512]{1,0:T(8,128)S(1)}, u32[]{:S(2)}, u32[]{:S(2)}) %collective-permute-start.4) | collective-permute-done | bytes 1048608 | tf_op jit(solution)/shard_map/ppermute | solution.py:199
  93.9 0.0 copy-start.2
  93.9 1.0 copy-done.2
  94.9 0.0 collective-permute-done.5.lower_ref
  94.9 0.0 collective-permute-done.3
  94.9 0.0 copy-start.4
  94.9 1.0 copy-done.4
  95.8 3.5 %all-to-all-start.4 = ((f32[4,128,512]{2,1,0:T(8,128)}), f32[4,128,512]{2,1,0:T(8,128)S(1)}, u32[]{:S(2)}, u32[]{:S(2)}) async-start(f32[4,128,512]{2,1,0:T(8,128)} %bitcast.7), calls=%async_computation.4 | async-start | bytes 2097152 | tf_op jit(solution)/shard_map/all_to_all | solution.py:226
  99.4 0.1 pad_add_fusion.at_ref
  99.4 0.0 copy-done.1
  99.4 0.0 copy-start.5
  99.4 1.2 copy-done.5
  100.7 8.0 %shard_map.60 = f32[1024,512]{1,0:T(8,128)} custom-call(s32[3]{0:T(128)S(1)} %pad_add_fusion.at_ref, f32[1024,512]{1,0:T(8,128)S(1)} %copy-done.1, f32[1024,1024]{1,0:T(8,128)} %panel_ref.3, f32[4,2,64,512]{3,2,1,0:T(8,128)} %bitcast.11.mine_ref, f32[4,2,64,512]{3,2,1,0:T(8,128)S(1)} %bitcast.21), custom_call_target="tpu_custom_call" | custom-call | flops 3221225472 | bytes 10485760 | tf_op jit(solution)/shard_map/pallas_call | solution.py:105
  108.6 3.1 %all-to-all-done.4 = f32[4,128,512]{2,1,0:T(8,128)S(1)} async-done(((f32[4,128,512]{2,1,0:T(8,128)}), f32[4,128,512]{2,1,0:T(8,128)S(1)}, u32[]{:S(2)}, u32[]{:S(2)}) %all-to-all-start.4) | async-done | bytes 1048608 | tf_op jit(solution)/shard_map/all_to_all | solution.py:226
  111.8 3.6 %collective-permute-start.6 = (f32[512,512]{1,0:T(8,128)S(1)}, f32[512,512]{1,0:T(8,128)S(1)}, u32[]{:S(2)}, u32[]{:S(2)}) collective-permute-start(f32[512,512]{1,0:T(8,128)S(1)} %bitcast.18), channel_id=1, source_target_pairs={{0,4},{4,0},{8,12},{12,8},{16,20},{20,16},{24,28},{28,24},{32,36},... | collective-permute-start | bytes 3145736 | tf_op jit(solution)/shard_map/ppermute | solution.py:196
  115.4 2.3 %collective-permute-done.6 = f32[512,512]{1,0:T(8,128)S(1)} collective-permute-done((f32[512,512]{1,0:T(8,128)S(1)}, f32[512,512]{1,0:T(8,128)S(1)}, u32[]{:S(2)}, u32[]{:S(2)}) %collective-permute-start.6) | collective-permute-done | bytes 1048608 | tf_op jit(solution)/shard_map/ppermute | solution.py:196
  117.7 0.0 copy-start.3
  117.7 1.2 copy-done.3
  118.9 8.0 %shard_map.61 = f32[2,128,1024]{2,1,0:T(8,128)} custom-call(s32[3]{0:T(128)S(1)} %pad_add_fusion.at_ref, f32[4,2,64,512]{3,2,1,0:T(8,128)S(1)} %bitcast.19, f32[4,2,64,512]{3,2,1,0:T(8,128)S(1)} %bitcast.22, f32[1024,512]{1,0:T(8,128)} %own_ref.1, f32[1024,512]{1,0:T(8,128)} %collective-permute-done.1.left_ref, ...), custom_call_target="tpu_custom_call" | custom-call | flops 3221225472 | bytes 12582912 | tf_op jit(solution)/shard_map/pallas_call | solution.py:168
  (2 shorter events, 0.0 us)
Async XLA Ops:
  0.6 1.6 %copy-start = (f32[1024,512]{1,0:T(8,128)S(1)}, f32[1024,512]{1,0:T(8,128)}, u32[]{:S(2)}) copy-start(f32[1024,512]{1,0:T(8,128)} %cot_ref.3) | copy-start | bytes 6291460
  7.0 6.0 %collective-permute-start = (f32[512,512]{1,0:T(8,128)S(1)}, f32[512,512]{1,0:T(8,128)S(1)}, u32[]{:S(2)}, u32[]{:S(2)}) collective-permute-start(f32[512,512]{1,0:T(8,128)S(1)} %bitcast.20), channel_id=1, source_target_pairs={{0,4},{4,0},{8,12},{12,8},{16,20},{20,16},{24,28},{28,24},{32,36},... | collective-permute-start | bytes 3145736 | tf_op jit(solution)/shard_map/ppermute | solution.py:196
  10.3 48.7 %collective-permute-start.1 = (f32[1024,512]{1,0:T(8,128)}, f32[1024,512]{1,0:T(8,128)}, u32[]{:S(2)}, u32[]{:S(2)}) collective-permute-start(f32[1024,512]{1,0:T(8,128)} %own_ref.1), channel_id=1, source_target_pairs={{0,1},{1,2},{2,3},{3,0},{4,5},{5,6},{6,7},{7,4},{8,9},{9,10},{10,1... | collective-permute-start | bytes 6291464 | tf_op jit(solution)/shard_map/ppermute | solution.py:199
  10.3 51.0 %collective-permute-start.2 = (f32[1024,512]{1,0:T(8,128)}, f32[1024,512]{1,0:T(8,128)}, u32[]{:S(2)}, u32[]{:S(2)}) collective-permute-start(f32[1024,512]{1,0:T(8,128)} %own_ref.1), channel_id=1, source_target_pairs={{0,3},{1,0},{2,1},{3,2},{4,7},{5,4},{6,5},{7,6},{8,11},{9,8},{10,9... | collective-permute-start | bytes 6291464 | tf_op jit(solution)/shard_map/ppermute | solution.py:202
  47.7 16.0 %all-to-all-start.2 = ((f32[8,16,512]{2,1,0:T(8,128)}), f32[8,16,512]{2,1,0:T(8,128)S(1)}, u32[]{:S(2)}, u32[]{:S(2)}) async-start(f32[8,16,512]{2,1,0:T(8,128)} %broadcast_in_dim.14), calls=%async_computation.2 | async-start | bytes 524288 | tf_op jit(solution)/shard_map/all_to_all | solution.py:212
  64.8 34.7 %copy-start.1 = (f32[1024,512]{1,0:T(8,128)S(1)}, f32[1024,512]{1,0:T(8,128)}, u32[]{:S(2)}) copy-start(f32[1024,512]{1,0:T(8,128)} %cot_ref.3) | copy-start | bytes 6291460
  64.8 18.1 %all-to-all-start.3 = ((f32[4,128,512]{2,1,0:T(8,128)}), f32[4,128,512]{2,1,0:T(8,128)}, u32[]{:S(2)}, u32[]{:S(2)}) async-start(f32[4,128,512]{2,1,0:T(8,128)} %broadcast_in_dim.15), calls=%async_computation.3 | async-start | bytes 2097152 | tf_op jit(solution)/shard_map/all_to_all | solution.py:212
  69.2 24.7 %collective-permute-start.4 = (f32[512,512]{1,0:T(8,128)}, f32[512,512]{1,0:T(8,128)S(1)}, u32[]{:S(2)}, u32[]{:S(2)}) collective-permute-start(f32[512,512]{1,0:T(8,128)} %slice.18), channel_id=1, source_target_pairs={{0,1},{1,2},{2,3},{3,0},{4,5},{5,6},{6,7},{7,4},{8,9},{9,10},{10,1... | collective-permute-start | bytes 3145736 | tf_op jit(solution)/shard_map/ppermute | solution.py:199
  69.3 25.6 %collective-permute-start.5 = (f32[512,512]{1,0:T(8,128)}, f32[512,512]{1,0:T(8,128)}, u32[]{:S(2)}, u32[]{:S(2)}) collective-permute-start(f32[512,512]{1,0:T(8,128)} %slice.19), channel_id=1, source_target_pairs={{0,3},{1,0},{2,1},{3,2},{4,7},{5,4},{6,5},{7,6},{8,11},{9,8},{10,9... | collective-permute-start | bytes 3145736 | tf_op jit(solution)/shard_map/ppermute | solution.py:202
  82.9 11.9 %collective-permute-start.3 = (f32[512,512]{1,0:T(8,128)}, f32[512,512]{1,0:T(8,128)S(1)}, u32[]{:S(2)}, u32[]{:S(2)}) collective-permute-start(f32[512,512]{1,0:T(8,128)} %bitcast.6), channel_id=1, source_target_pairs={{0,4},{4,0},{8,12},{12,8},{16,20},{20,16},{24,28},{28,24},{32,36},... | collective-permute-start | bytes 3145736 | tf_op jit(solution)/shard_map/ppermute | solution.py:196
  93.9 1.0 copy-start.2
  94.9 1.0 copy-start.4
  95.8 15.9 %all-to-all-start.4 = ((f32[4,128,512]{2,1,0:T(8,128)}), f32[4,128,512]{2,1,0:T(8,128)S(1)}, u32[]{:S(2)}, u32[]{:S(2)}) async-start(f32[4,128,512]{2,1,0:T(8,128)} %bitcast.7), calls=%async_computation.4 | async-start | bytes 2097152 | tf_op jit(solution)/shard_map/all_to_all | solution.py:226
  99.4 1.2 copy-start.5
  111.8 5.9 %collective-permute-start.6 = (f32[512,512]{1,0:T(8,128)S(1)}, f32[512,512]{1,0:T(8,128)S(1)}, u32[]{:S(2)}, u32[]{:S(2)}) collective-permute-start(f32[512,512]{1,0:T(8,128)S(1)} %bitcast.18), channel_id=1, source_target_pairs={{0,4},{4,0},{8,12},{12,8},{16,20},{20,16},{24,28},{28,24},{32,36},... | collective-permute-start | bytes 3145736 | tf_op jit(solution)/shard_map/ppermute | solution.py:196
  117.7 1.2 copy-start.3

commit v3 on v2

--- a/solution.py
+++ b/solution.py
@@ -11,7 +11,7 @@
 NZ, NY, NX = 8, 4, 4
 CHIPS = NZ * NY
 ROOT = 2 * CHIPS - 1
-VMEM_LIMIT = 48 * 1024 * 1024
+VMEM_LIMIT = 60 * 1024 * 1024
 
 
 def rank(z, y, c):
@@ -217,11 +217,10 @@
     mine = jnp.where(c == 1, kept.reshape(bs, cols), swap(given.reshape(bs, cols)))
     mine = scatter(scatter(mine, ALONG_Y), ALONG_Z)
     mine = gather(mine, ALONG_Z)
-    upper, lower = from_left[: local_rows // 2], from_right[local_rows // 2 :]
+    upper, lower = right(from_left[: local_rows // 2]), left(from_right[local_rows // 2 :])
+    mine = gather(mine, ALONG_Y)
     mine, upper, lower = lax.optimization_barrier((mine, upper, lower))
-    upper, lower = right(upper), left(lower)
-    mine = gather(mine, ALONG_Y)
-    mine, other, upper, lower = lax.optimization_barrier((mine, swap(mine), upper, lower))
+    other = swap(mine)
 
     wide = lax.all_to_all(mine.reshape(4, STEPS * half, cols), "cols", 0, 0)
     shape = (4, STEPS, half, cols)

time: 128 us -> 121 us (0.945)
  local copies, waits for them, and re-layouts: 12.4 us -> 6.38 us
  Pallas kernels: 20.7 us -> 24.9 us
  starting transfers between devices: 26.1 us -> 22 us
  waiting for transfers between devices: 32.9 us -> 30.7 us
  other arithmetic: 0.31 us -> 1.99 us
    all_to_all x2, waiting for transfers between devices: 11 us -> 0.01 us  [gather(): lax.all_to_all(blocks, 'rows', 0, 0, axis_index_groups=groups)]
    ppermute x2, waiting for transfers between devices: 16.5 us -> 22.4 us  [right(): return lax.ppermute(x, 'cols', X_RIGHT)]
    ppermute x3, starting transfers between devices: 9.31 us -> 5.98 us  [swap(): return lax.ppermute(x, 'rows', SWAP)]
    slice x2, local copies, waits for them, and re-layouts: 4.6 us -> 1.36 us  [the longest x1 1.29 us: on_device(): from_right[local_rows // 2:]]
    unnamed x12 -> x10, local copies, waits for them, and re-layouts: 5.99 us -> 3.16 us
    pallas_call x1, Pallas kernels: 4.78 us -> 6.72 us  [solve(): pl.pallas_call(solve_kernel, grid=(1,), in_specs=[pl.BlockSpec((rows, col...]
    all_to_all x1, waiting for transfers between devices: 3.14 us -> 4.63 us  [on_device(): wide = lax.all_to_all(mine.reshape(4, STEPS * half, cols), 'cols', 0, 0)]
    pallas_call x1, Pallas kernels: 7.98 us -> 9.42 us  [grad(): pl.pallas_call(grad_kernel, grid_spec=pltpu.PrefetchScalarGridSpec(num_sc...]
  transfers between devices with their start and end apart: 10 -> 10, of which waited for: 5 -> 5; matrix products, arithmetic and copies ran while one was open for 4% -> 4% of each run, Pallas kernels for 6% -> 7%
where the time goes in v3:
time: 121 us; the launch traced here: 120 us
  blocking collectives  33.7 us (28%)
  waiting for transfers between devices  30.7 us (25%)
  Pallas kernels  24.9 us (21%)
  starting transfers between devices  22 us (18%)
  local copies, waits for them, and re-layouts  6.38 us (5%)
  other arithmetic  1.99 us (2%)
    all_to_all x2, blocking collectives, scatter(): lax.all_to_all(blocks, 'rows', 0, 0, axis_index_groups=groups)[count - 1]  33.7 us
    ppermute x2, waiting for transfers between devices, right(): return lax.ppermute(x, 'cols', X_RIGHT)  22.4 us
    pallas_call x1, Pallas kernels, grad(): pl.pallas_call(grad_kernel, grid_spec=pltpu.PrefetchScalarGridSpec(num_sc...  9.42 us
    pallas_call x1, Pallas kernels, update(): pl.pallas_call(update_kernel, grid_spec=pltpu.PrefetchScalarGridSpec(num_...  8.77 us
    all_to_all x2, starting transfers between devices, gather(): lax.all_to_all(blocks, 'rows', 0, 0, axis_index_groups=groups)  7.67 us
    pallas_call x1, Pallas kernels, solve(): pl.pallas_call(solve_kernel, grid=(1,), in_specs=[pl.BlockSpec((rows, col...  6.72 us
    ppermute x3, starting transfers between devices, swap(): return lax.ppermute(x, 'rows', SWAP)  5.98 us
    all_to_all x1, waiting for transfers between devices, on_device(): wide = lax.all_to_all(mine.reshape(4, STEPS * half, cols), 'cols', 0, 0)  4.63 us
  transfers between devices with their start and end apart: 10, of which 5 were waited for; matrix products, arithmetic and copies ran while one was open for 4% of the time, Pallas kernels for 7%

profile of v3, /device:TPU:1, one launch (start us, length us, event | category | flops | bytes accessed | tf_op | source)
XLA Modules:
  0.0 120.3 jit_solution(15596047670075847484)
XLA Ops:
  0.6 6.7 %shard_map.59 = (f32[4,2,64,512]{3,2,1,0:T(8,128)}, f32[4,2,64,512]{3,2,1,0:T(8,128)}) custom-call(f32[1024,512]{1,0:T(8,128)} %cot_ref.3, f32[1024,1024]{1,0:T(8,128)} %panel_ref.3, f32[2,512,512]{2,1,0:T(8,128)} %dinv_ref.1), custom_call_target="tpu_custom_call" | custom-call | flops 2415919104 | bytes 7340032 | tf_op jit(solution)/shard_map/pallas_call | solution.py:59
  7.4 3.2 %collective-permute-start = (f32[512,512]{1,0:T(8,128)}, f32[512,512]{1,0:T(8,128)S(1)}, u32[]{:S(2)}, u32[]{:S(2)}) collective-permute-start(f32[512,512]{1,0:T(8,128)} %bitcast.23), channel_id=1, source_target_pairs={{0,4},{4,0},{8,12},{12,8},{16,20},{20,16},{24,28},{28,24},{32,36},... | collective-permute-start | bytes 3145736 | tf_op jit(solution)/shard_map/ppermute | solution.py:196
  10.6 0.0 collective-permute-start.1
  10.6 2.7 %collective-permute-start.3 = (f32[1024,512]{1,0:T(8,128)}, f32[1024,512]{1,0:T(8,128)}, u32[]{:S(2)}, u32[]{:S(2)}) collective-permute-start(f32[1024,512]{1,0:T(8,128)} %own_ref.1), channel_id=1, source_target_pairs={{0,3},{1,0},{2,1},{3,2},{4,7},{5,4},{6,5},{7,6},{8,11},{9,8},{10,9... | collective-permute-start | bytes 6291464 | tf_op jit(solution)/shard_map/ppermute | solution.py:202
  13.3 0.0 collective-permute-done
  13.3 1.4 %bitcast_select_fusion = f32[512,512]{1,0:T(8,128)S(1)} fusion(f32[512,512]{1,0:T(8,128)S(1)} %collective-permute-done, f32[4,2,64,512]{3,2,1,0:T(8,128)} %get-tuple-element.9, pred[]{:T(512)S(6)} %eq.5), kind=kLoop, calls=%fused_computation | loop fusion | flops 262144 | bytes 3145729 | tf_op jit(solution)/shard_map/jit(_where)/select_n | solution.py:217
  14.7 16.6 %all_to_all.25 = f32[4,128,512]{2,1,0:T(8,128)S(1)} all-to-all(f32[4,128,512]{2,1,0:T(8,128)S(1)} %bitcast.18), channel_id=1, replica_groups={{0,8,16,24},{4,12,20,28},{32,40,48,56},{36,44,52,60},{64,72,80,88},{68,..., dimensions={0} | all-to-all | bytes 2097152 | tf_op jit(solution)/shard_map/all_to_all | solution.py:207
  31.4 17.1 %all_to_all.26 = f32[8,16,512]{2,1,0:T(8,128)S(1)} all-to-all(f32[8,16,512]{2,1,0:T(8,128)S(1)} %bitcast.22), channel_id=1, replica_groups={{0,32,64,96,128,160,192,224},{4,36,68,100,132,164,196,228},{8,40,72,104..., dimensions={0} | all-to-all | bytes 524288 | tf_op jit(solution)/shard_map/all_to_all | solution.py:207
  48.5 0.7 broadcast_in_dim.15
  49.2 3.4 %all-to-all-start.2 = ((f32[8,16,512]{2,1,0:T(8,128)}), f32[8,16,512]{2,1,0:T(8,128)S(1)}, u32[]{:S(2)}, u32[]{:S(2)}) async-start(f32[8,16,512]{2,1,0:T(8,128)} %broadcast_in_dim.15), calls=%async_computation.2 | async-start | bytes 524288 | tf_op jit(solution)/shard_map/all_to_all | solution.py:212
  52.6 6.7 %collective-permute-done.1.left_ref = f32[1024,512]{1,0:T(8,128)S(1)} collective-permute-done((f32[1024,512]{1,0:T(8,128)}, f32[1024,512]{1,0:T(8,128)S(1)}, u32[]{:S(2)}, u32[]{:S(2)}) %collective-permute-start.1) | collective-permute-done | bytes 2097184 | tf_op jit(solution)/shard_map/ppermute | solution.py:199
  59.3 0.0 copy-start.1
  59.3 0.1 slice.18
  59.4 0.1 collective-permute-start.2
  59.4 1.2 copy-done.1
  60.6 0.0 collective-permute-done.3.right_ref
  60.6 1.3 %slice.19 = f32[512,512]{1,0:T(8,128)S(1)} slice(f32[1024,512]{1,0:T(8,128)} %collective-permute-done.3.right_ref), slice={[512:1024], [0:512]} | slice | bytes 2097152 | tf_op jit(solution)/shard_map/slice | solution.py:220
  61.9 1.6 %collective-permute-start.4 = (f32[512,512]{1,0:T(8,128)S(1)}, f32[512,512]{1,0:T(8,128)S(1)}, u32[]{:S(2)}, u32[]{:S(2)}) collective-permute-start(f32[512,512]{1,0:T(8,128)S(1)} %slice.19), channel_id=1, source_target_pairs={{0,3},{1,0},{2,1},{3,2},{4,7},{5,4},{6,5},{7,6},{8,11},{9,8},{10,9... | collective-permute-start | bytes 3145736 | tf_op jit(solution)/shard_map/ppermute | solution.py:202
  63.5 0.0 all-to-all-done.2
  63.5 1.1 broadcast_in_dim.17
  64.6 4.3 %all-to-all-start.3 = ((f32[4,128,512]{2,1,0:T(8,128)}), f32[4,128,512]{2,1,0:T(8,128)}, u32[]{:S(2)}, u32[]{:S(2)}) async-start(f32[4,128,512]{2,1,0:T(8,128)} %broadcast_in_dim.17), calls=%async_computation.3 | async-start | bytes 2097152 | tf_op jit(solution)/shard_map/all_to_all | solution.py:212
  68.9 15.8 %collective-permute-done.2.upper_ref = f32[512,512]{1,0:T(8,128)} collective-permute-done((f32[512,512]{1,0:T(8,128)S(1)}, f32[512,512]{1,0:T(8,128)}, u32[]{:S(2)}, u32[]{:S(2)}) %collective-permute-start.2) | collective-permute-done | bytes 1048608 | tf_op jit(solution)/shard_map/ppermute | solution.py:199
  84.6 1.3 %collective-permute-done.4.lower_ref = f32[512,512]{1,0:T(8,128)S(1)} collective-permute-done((f32[512,512]{1,0:T(8,128)S(1)}, f32[512,512]{1,0:T(8,128)S(1)}, u32[]{:S(2)}, u32[]{:S(2)}) %collective-permute-start.4) | collective-permute-done | bytes 1048608 | tf_op jit(solution)/shard_map/ppermute | solution.py:202
  85.9 0.0 copy-start.2
  85.9 0.0 all-to-all-done.3
  85.9 1.6 %collective-permute-start.5 = (f32[512,512]{1,0:T(8,128)}, f32[512,512]{1,0:T(8,128)S(1)}, u32[]{:S(2)}, u32[]{:S(2)}) collective-permute-start(f32[512,512]{1,0:T(8,128)} %bitcast.6), channel_id=1, source_target_pairs={{0,4},{4,0},{8,12},{12,8},{16,20},{20,16},{24,28},{28,24},{32,36},... | collective-permute-start | bytes 3145736 | tf_op jit(solution)/shard_map/ppermute | solution.py:196
  87.6 4.0 %all-to-all-start.4 = ((f32[4,128,512]{2,1,0:T(8,128)}), f32[4,128,512]{2,1,0:T(8,128)S(1)}, u32[]{:S(2)}, u32[]{:S(2)}) async-start(f32[4,128,512]{2,1,0:T(8,128)} %bitcast.7), calls=%async_computation.4 | async-start | bytes 2097152 | tf_op jit(solution)/shard_map/all_to_all | solution.py:225
  91.5 0.6 pad_add_fusion.at_ref
  92.1 0.0 collective-permute-done.5
  92.1 0.0 copy-start.3
  92.1 1.0 copy-done.3
  93.1 8.8 %shard_map.60 = f32[1024,512]{1,0:T(8,128)} custom-call(s32[3]{0:T(128)} %pad_add_fusion.at_ref, f32[1024,512]{1,0:T(8,128)} %cot_ref.3, f32[1024,1024]{1,0:T(8,128)} %panel_ref.3, f32[4,2,64,512]{3,2,1,0:T(8,128)} %bitcast.11.mine_ref, f32[4,2,64,512]{3,2,1,0:T(8,128)} %bitcast.24), custom_call_target="tpu_custom_call" | custom-call | flops 3221225472 | bytes 10485760 | tf_op jit(solution)/shard_map/pallas_call | solution.py:105
  101.8 0.0 copy-done.2
  101.9 4.6 %all-to-all-done.4 = f32[4,128,512]{2,1,0:T(8,128)S(1)} async-done(((f32[4,128,512]{2,1,0:T(8,128)}), f32[4,128,512]{2,1,0:T(8,128)S(1)}, u32[]{:S(2)}, u32[]{:S(2)}) %all-to-all-start.4) | async-done | bytes 1048608 | tf_op jit(solution)/shard_map/all_to_all | solution.py:225
  106.5 0.0 copy-start
  106.5 1.1 collective-permute-start.6
  107.6 2.3 %collective-permute-done.6 = f32[512,512]{1,0:T(8,128)S(1)} collective-permute-done((f32[512,512]{1,0:T(8,128)S(1)}, f32[512,512]{1,0:T(8,128)S(1)}, u32[]{:S(2)}, u32[]{:S(2)}) %collective-permute-start.6) | collective-permute-done | bytes 1048608 | tf_op jit(solution)/shard_map/ppermute | solution.py:196
  109.9 0.0 copy-start.4
  109.9 0.0 copy-done
  109.9 1.0 copy-done.4
  110.9 9.4 %shard_map.61 = f32[2,128,1024]{2,1,0:T(8,128)} custom-call(s32[3]{0:T(128)} %pad_add_fusion.at_ref, f32[4,2,64,512]{3,2,1,0:T(8,128)} %bitcast.21, f32[4,2,64,512]{3,2,1,0:T(8,128)} %bitcast.25, f32[1024,512]{1,0:T(8,128)} %own_ref.1, f32[1024,512]{1,0:T(8,128)} %copy-done.1, f32[1024,512]{1,0:T(8,128)} %collective-permute-done.3.right_ref, ...), custom_call_target="tpu_custom_call" | custom-call | flops 3221225472 | bytes 12582912 | tf_op jit(solution)/shard_map/pallas_call | solution.py:168
  (2 shorter events, 0.0 us)
Async XLA Ops:
  7.4 5.9 %collective-permute-start = (f32[512,512]{1,0:T(8,128)}, f32[512,512]{1,0:T(8,128)S(1)}, u32[]{:S(2)}, u32[]{:S(2)}) collective-permute-start(f32[512,512]{1,0:T(8,128)} %bitcast.23), channel_id=1, source_target_pairs={{0,4},{4,0},{8,12},{12,8},{16,20},{20,16},{24,28},{28,24},{32,36},... | collective-permute-start | bytes 3145736 | tf_op jit(solution)/shard_map/ppermute | solution.py:196
  10.6 48.7 %collective-permute-start.1 = (f32[1024,512]{1,0:T(8,128)}, f32[1024,512]{1,0:T(8,128)S(1)}, u32[]{:S(2)}, u32[]{:S(2)}) collective-permute-start(f32[1024,512]{1,0:T(8,128)} %own_ref.1), channel_id=1, source_target_pairs={{0,1},{1,2},{2,3},{3,0},{4,5},{5,6},{6,7},{7,4},{8,9},{9,10},{10,1... | collective-permute-start | bytes 6291464 | tf_op jit(solution)/shard_map/ppermute | solution.py:199
  10.6 50.0 %collective-permute-start.3 = (f32[1024,512]{1,0:T(8,128)}, f32[1024,512]{1,0:T(8,128)}, u32[]{:S(2)}, u32[]{:S(2)}) collective-permute-start(f32[1024,512]{1,0:T(8,128)} %own_ref.1), channel_id=1, source_target_pairs={{0,3},{1,0},{2,1},{3,2},{4,7},{5,4},{6,5},{7,6},{8,11},{9,8},{10,9... | collective-permute-start | bytes 6291464 | tf_op jit(solution)/shard_map/ppermute | solution.py:202
  49.2 14.3 %all-to-all-start.2 = ((f32[8,16,512]{2,1,0:T(8,128)}), f32[8,16,512]{2,1,0:T(8,128)S(1)}, u32[]{:S(2)}, u32[]{:S(2)}) async-start(f32[8,16,512]{2,1,0:T(8,128)} %broadcast_in_dim.15), calls=%async_computation.2 | async-start | bytes 524288 | tf_op jit(solution)/shard_map/all_to_all | solution.py:212
  59.3 1.3 %copy-start.1 = (f32[1024,512]{1,0:T(8,128)}, f32[1024,512]{1,0:T(8,128)S(1)}, u32[]{:S(2)}) copy-start(f32[1024,512]{1,0:T(8,128)S(1)} %collective-permute-done.1.left_ref) | copy-start | bytes 6291460
  59.4 25.3 %collective-permute-start.2 = (f32[512,512]{1,0:T(8,128)S(1)}, f32[512,512]{1,0:T(8,128)}, u32[]{:S(2)}, u32[]{:S(2)}) collective-permute-start(f32[512,512]{1,0:T(8,128)S(1)} %slice.18), channel_id=1, source_target_pairs={{0,1},{1,2},{2,3},{3,0},{4,5},{5,6},{6,7},{7,4},{8,9},{9,10},{10,1... | collective-permute-start | bytes 3145736 | tf_op jit(solution)/shard_map/ppermute | solution.py:199
  61.9 24.0 %collective-permute-start.4 = (f32[512,512]{1,0:T(8,128)S(1)}, f32[512,512]{1,0:T(8,128)S(1)}, u32[]{:S(2)}, u32[]{:S(2)}) collective-permute-start(f32[512,512]{1,0:T(8,128)S(1)} %slice.19), channel_id=1, source_target_pairs={{0,3},{1,0},{2,1},{3,2},{4,7},{5,4},{6,5},{7,6},{8,11},{9,8},{10,9... | collective-permute-start | bytes 3145736 | tf_op jit(solution)/shard_map/ppermute | solution.py:202
  64.6 21.3 %all-to-all-start.3 = ((f32[4,128,512]{2,1,0:T(8,128)}), f32[4,128,512]{2,1,0:T(8,128)}, u32[]{:S(2)}, u32[]{:S(2)}) async-start(f32[4,128,512]{2,1,0:T(8,128)} %broadcast_in_dim.17), calls=%async_computation.3 | async-start | bytes 2097152 | tf_op jit(solution)/shard_map/all_to_all | solution.py:212
  85.9 15.9 %copy-start.2 = (f32[512,512]{1,0:T(8,128)}, f32[512,512]{1,0:T(8,128)S(1)}, u32[]{:S(2)}) copy-start(f32[512,512]{1,0:T(8,128)S(1)} %collective-permute-done.4.lower_ref) | copy-start | bytes 3145732
  85.9 6.2 %collective-permute-start.5 = (f32[512,512]{1,0:T(8,128)}, f32[512,512]{1,0:T(8,128)S(1)}, u32[]{:S(2)}, u32[]{:S(2)}) collective-permute-start(f32[512,512]{1,0:T(8,128)} %bitcast.6), channel_id=1, source_target_pairs={{0,4},{4,0},{8,12},{12,8},{16,20},{20,16},{24,28},{28,24},{32,36},... | collective-permute-start | bytes 3145736 | tf_op jit(solution)/shard_map/ppermute | solution.py:196
  87.6 18.9 %all-to-all-start.4 = ((f32[4,128,512]{2,1,0:T(8,128)}), f32[4,128,512]{2,1,0:T(8,128)S(1)}, u32[]{:S(2)}, u32[]{:S(2)}) async-start(f32[4,128,512]{2,1,0:T(8,128)} %bitcast.7), calls=%async_computation.4 | async-start | bytes 2097152 | tf_op jit(solution)/shard_map/all_to_all | solution.py:225
  92.1 1.0 copy-start.3
  106.5 3.4 %copy-start = (f32[4,128,512]{2,1,0:T(8,128)}, f32[4,128,512]{2,1,0:T(8,128)S(1)}, u32[]{:S(2)}) copy-start(f32[4,128,512]{2,1,0:T(8,128)S(1)} %all-to-all-done.4) | copy-start | bytes 3145732
  106.5 3.4 %collective-permute-start.6 = (f32[512,512]{1,0:T(8,128)S(1)}, f32[512,512]{1,0:T(8,128)S(1)}, u32[]{:S(2)}, u32[]{:S(2)}) collective-permute-start(f32[512,512]{1,0:T(8,128)S(1)} %bitcast.20), channel_id=1, source_target_pairs={{0,4},{4,0},{8,12},{12,8},{16,20},{20,16},{24,28},{28,24},{32,36},... | collective-permute-start | bytes 3145736 | tf_op jit(solution)/shard_map/ppermute | solution.py:196
  109.9 1.0 copy-start.4

commit v4 on v3

--- a/solution.py
+++ b/solution.py
@@ -23,6 +23,7 @@
 ALONG_Z = [[rank(z, y, c) for z in range(NZ)] for y in range(NY) for c in range(2)]
 X_RIGHT = [(q, (q + 1) % NX) for q in range(NX)]
 X_LEFT = [(q, (q - 1) % NX) for q in range(NX)]
+X_ACROSS = [(q, (q + 2) % NX) for q in range(NX)]
 
 
 def split(x):
@@ -126,29 +127,30 @@
     )(at, cotangent, panel, mine, other)
 
 
-def grad_kernel(at_ref, mine_ref, other_ref, own_ref, left_ref, right_ref, upper_ref, lower_ref, out_ref, high, low):
+def grad_kernel(at_ref, *refs):
+    pairs, saved_refs, (out_ref, high, low) = refs[:8], refs[8:13], refs[13:]
+    own_ref, left_ref, right_ref, upper_ref, lower_ref = saved_refs
     i = pl.program_id(0)
     me, q, core = at_ref[0], at_ref[1], at_ref[2]
-    half = mine_ref.shape[2]
+    half = pairs[0].shape[2]
     quarter = 2 * half
     tile = out_ref.shape[2]
-    local_rows = 4 * tile
+    local_rows = 2 * tile
 
     @pl.when(i == 0)
     def _():
         for j in range(4):
             for k in range(STEPS):
-                a, b = mine_ref[j, k], other_ref[j, k]
+                a, b = pairs[2 * j][0, k], pairs[2 * j + 1][0, k]
                 for h in range(2):
                     at = pl.ds((k * 2 + h) * half, half)
                     high[j, at, :], low[j, at, :] = split(-jnp.where(core == h, a, b))
 
-    def term(away, saved):
-        j = lax.rem(q + away, NX)
+    def term(j, saved):
         return dot3((high[j], low[j]), split(saved), LAST)
 
-    total = term(0, own_ref[...]) + term(3, left_ref[...]) + term(1, right_ref[...])
-    total += term(2, jnp.where(i < 2, upper_ref[...], lower_ref[...]))
+    total = term(0, own_ref[...]) + term(1, left_ref[...]) + term(2, right_ref[...])
+    total += term(3, jnp.where(i == 0, upper_ref[...], lower_ref[...]))
     column = me * local_rows + i * tile + lax.broadcasted_iota(jnp.int32, (quarter, tile), 1)
     row = lax.broadcasted_iota(jnp.int32, (quarter, tile), 0) + q * quarter
     for k in range(STEPS):
@@ -157,30 +159,27 @@
         out_ref[k] = jnp.where(column <= limit, part, jnp.float32(0.0))
 
 
-def grad(at, mine, other, own, left, right, upper, lower):
+def grad(at, mine, other, near, own, left, right, upper, lower):
     _, _, half, cols = mine.shape
     rows = own.shape[0]
-    tile = rows // 4
-    halves = pl.BlockSpec(mine.shape, lambda i, at: (0, 0, 0, 0))
+    tile = rows // 2
+    mine_part = pl.BlockSpec((1, STEPS, half, cols), lambda i, at: (at[1], 0, 0, 0))
+    near_part = pl.BlockSpec((1, STEPS, half, cols), lambda i, at: (0, 0, 0, 0))
     tiled = pl.BlockSpec((tile, cols), lambda i, at: (i, 0))
-    first = pl.BlockSpec((tile, cols), lambda i, at: (jnp.minimum(i, 1), 0))
-    last = pl.BlockSpec((tile, cols), lambda i, at: (jnp.maximum(i - 2, 0), 0))
+    fixed = pl.BlockSpec((tile, cols), lambda i, at: (0, 0))
     return pl.pallas_call(
         grad_kernel,
         grid_spec=pltpu.PrefetchScalarGridSpec(
             num_scalar_prefetch=1,
-            grid=(4,),
-            in_specs=[halves, halves, tiled, tiled, tiled, first, last],
+            grid=(2,),
+            in_specs=[mine_part] * 2 + [near_part] * 6 + [tiled] * 3 + [fixed] * 2,
             out_specs=pl.BlockSpec((STEPS, 2 * half, tile), lambda i, at: (0, 0, i)),
-            scratch_shapes=[
-                pltpu.VMEM((4, STEPS * 2 * half, cols), jnp.bfloat16),
-                pltpu.VMEM((4, STEPS * 2 * half, cols), jnp.bfloat16),
-            ],
+            scratch_shapes=[pltpu.VMEM((4, STEPS * 2 * half, cols), jnp.bfloat16)] * 2,
         ),
         out_shape=jax.ShapeDtypeStruct((STEPS, 2 * half, rows), jnp.float32),
         compiler_params=pltpu.CompilerParams(vmem_limit_bytes=VMEM_LIMIT),
         cost_estimate=pl.CostEstimate(flops=96 * half * rows * cols, bytes_accessed=12 << 20, transcendentals=0),
-    )(at, mine, other, own, left, right, upper, lower)
+    )(at, mine, other, *near, own, left, right, upper, lower)
 
 
 def on_device(cotangent, saved, panel, dinv):
@@ -222,12 +221,16 @@
     mine, upper, lower = lax.optimization_barrier((mine, upper, lower))
     other = swap(mine)
 
-    wide = lax.all_to_all(mine.reshape(4, STEPS * half, cols), "cols", 0, 0)
+    def of_quarter(away):
+        n = STEPS * half
+        return lax.dynamic_slice_in_dim(mine, lax.rem(q + away, NX) * n, n, 0)
+
+    near = [right(of_quarter(1)), left(of_quarter(3)), lax.ppermute(of_quarter(2), "cols", X_ACROSS)]
     shape = (4, STEPS, half, cols)
     carried = update(at, cotangent, panel, mine.reshape(shape), other.reshape(shape))
-    wide, carried = lax.optimization_barrier((wide, carried))
-    other = swap(wide.reshape(4 * STEPS * half, cols))
-    factor = grad(at, wide.reshape(shape), other.reshape(shape), saved, from_left, from_right, upper, lower)
+    near, carried = lax.optimization_barrier((near, carried))
+    near = [part.reshape(1, STEPS, half, cols) for rows in near for part in (rows, swap(rows))]
+    factor = grad(at, mine.reshape(shape), other.reshape(shape), near, saved, from_left, from_right, upper, lower)
     return carried, factor
 
 

time: 121 us -> 120 us (level)
  waiting for transfers between devices: 30.7 us -> 27.4 us
  local copies, waits for them, and re-layouts: 6.38 us -> 7.91 us
    all_to_all x1 -> x0, waiting for transfers between devices: 4.63 us -> none  [on_device(): wide = lax.all_to_all(mine.reshape(4, STEPS * half, cols), 'cols', 0, 0)]
    all_to_all x1 -> x0, starting transfers between devices: 3.99 us -> none  [on_device(): wide = lax.all_to_all(mine.reshape(4, STEPS * half, cols), 'cols', 0, 0)]
    ppermute x2 -> x3, starting transfers between devices: 4.26 us -> 6.84 us  [left(): return lax.ppermute(x, 'cols', X_LEFT)]
    ppermute x2 -> x3, waiting for transfers between devices: 1.28 us -> 3.58 us  [left(): return lax.ppermute(x, 'cols', X_LEFT)]
    ppermute x0 -> x1, starting transfers between devices: none -> 1.92 us  [on_device(): lax.ppermute(of_quarter(2), 'cols', X_ACROSS)]
    unnamed x10 -> x20, local copies, waits for them, and re-layouts: 3.16 us -> 1.78 us
    ppermute x3 -> x5, starting transfers between devices: 5.98 us -> 6.82 us  [swap(): return lax.ppermute(x, 'rows', SWAP)]
    ppermute x2 -> x3, waiting for transfers between devices: 22.4 us -> 22.4 us  [right(): return lax.ppermute(x, 'cols', X_RIGHT)]
  transfers between devices with their start and end apart: 10 -> 14, of which waited for: 5 -> 7; matrix products, arithmetic and copies ran while one was open for 4% -> 7% of each run, Pallas kernels for 7% -> 7%
where the time goes in v4:
time: 120 us; the launch traced here: 119 us
  blocking collectives  33.7 us (28%)
  waiting for transfers between devices  27.4 us (23%)
  Pallas kernels  24.5 us (20%)
  starting transfers between devices  23.1 us (19%)
  local copies, waits for them, and re-layouts  7.91 us (7%)
  other arithmetic  2.02 us (2%)
    all_to_all x2, blocking collectives, scatter(): lax.all_to_all(blocks, 'rows', 0, 0, axis_index_groups=groups)[count - 1]  33.7 us
    ppermute x3, waiting for transfers between devices, right(): return lax.ppermute(x, 'cols', X_RIGHT)  22.4 us
    pallas_call x1, Pallas kernels, grad(): pl.pallas_call(grad_kernel, grid_spec=pltpu.PrefetchScalarGridSpec(num_sc...  9.04 us
    pallas_call x1, Pallas kernels, update(): pl.pallas_call(update_kernel, grid_spec=pltpu.PrefetchScalarGridSpec(num_...  8.78 us
    all_to_all x2, starting transfers between devices, gather(): lax.all_to_all(blocks, 'rows', 0, 0, axis_index_groups=groups)  6.93 us
    ppermute x3, starting transfers between devices, left(): return lax.ppermute(x, 'cols', X_LEFT)  6.84 us
    ppermute x5, starting transfers between devices, swap(): return lax.ppermute(x, 'rows', SWAP)  6.82 us
    pallas_call x1, Pallas kernels, solve(): pl.pallas_call(solve_kernel, grid=(1,), in_specs=[pl.BlockSpec((rows, col...  6.72 us
  transfers between devices with their start and end apart: 14, of which 7 were waited for; matrix products, arithmetic and copies ran while one was open for 7% of the time, Pallas kernels for 7%

profile of v4, /device:TPU:1, one launch (start us, length us, event | category | flops | bytes accessed | tf_op | source)
XLA Modules:
  0.0 119.4 jit_solution(339864105103939752)
XLA Ops:
  0.6 6.7 %shard_map.59 = (f32[4,2,64,512]{3,2,1,0:T(8,128)}, f32[4,2,64,512]{3,2,1,0:T(8,128)}) custom-call(f32[1024,512]{1,0:T(8,128)} %cot_ref.3, f32[1024,1024]{1,0:T(8,128)} %panel_ref.3, f32[2,512,512]{2,1,0:T(8,128)} %dinv_ref.1), custom_call_target="tpu_custom_call" | custom-call | flops 2415919104 | bytes 7340032 | tf_op jit(solution)/shard_map/pallas_call | solution.py:60
  7.3 3.2 %collective-permute-start = (f32[512,512]{1,0:T(8,128)}, f32[512,512]{1,0:T(8,128)S(1)}, u32[]{:S(2)}, u32[]{:S(2)}) collective-permute-start(f32[512,512]{1,0:T(8,128)} %bitcast.35), channel_id=1, source_target_pairs={{0,4},{4,0},{8,12},{12,8},{16,20},{20,16},{24,28},{28,24},{32,36},... | collective-permute-start | bytes 3145736 | tf_op jit(solution)/shard_map/ppermute | solution.py:195
  10.6 0.0 collective-permute-start.1
  10.6 2.7 %collective-permute-start.3 = (f32[1024,512]{1,0:T(8,128)}, f32[1024,512]{1,0:T(8,128)}, u32[]{:S(2)}, u32[]{:S(2)}) collective-permute-start(f32[1024,512]{1,0:T(8,128)} %refs_8_.1), channel_id=1, source_target_pairs={{0,3},{1,0},{2,1},{3,2},{4,7},{5,4},{6,5},{7,6},{8,11},{9,8},{10,9... | collective-permute-start | bytes 6291464 | tf_op jit(solution)/shard_map/ppermute | solution.py:201
  13.3 0.0 collective-permute-done
  13.3 1.4 %bitcast_select_fusion = f32[512,512]{1,0:T(8,128)S(1)} fusion(f32[512,512]{1,0:T(8,128)S(1)} %collective-permute-done, f32[4,2,64,512]{3,2,1,0:T(8,128)} %get-tuple-element.11, pred[]{:T(512)S(6)} %eq.5), kind=kLoop, calls=%fused_computation | loop fusion | flops 262144 | bytes 3145729 | tf_op jit(solution)/shard_map/jit(_where)/select_n | solution.py:216
  14.7 16.6 %all_to_all.20 = f32[4,128,512]{2,1,0:T(8,128)S(1)} all-to-all(f32[4,128,512]{2,1,0:T(8,128)S(1)} %bitcast.24), channel_id=1, replica_groups={{0,8,16,24},{4,12,20,28},{32,40,48,56},{36,44,52,60},{64,72,80,88},{68,..., dimensions={0} | all-to-all | bytes 2097152 | tf_op jit(solution)/shard_map/all_to_all | solution.py:206
  31.4 17.1 %all_to_all.21 = f32[8,16,512]{2,1,0:T(8,128)S(1)} all-to-all(f32[8,16,512]{2,1,0:T(8,128)S(1)} %bitcast.28), channel_id=1, replica_groups={{0,32,64,96,128,160,192,224},{4,36,68,100,132,164,196,228},{8,40,72,104..., dimensions={0} | all-to-all | bytes 524288 | tf_op jit(solution)/shard_map/all_to_all | solution.py:206
  48.5 0.7 broadcast_in_dim.15
  49.2 3.4 %all-to-all-start.2 = ((f32[8,16,512]{2,1,0:T(8,128)}), f32[8,16,512]{2,1,0:T(8,128)S(1)}, u32[]{:S(2)}, u32[]{:S(2)}) async-start(f32[8,16,512]{2,1,0:T(8,128)} %broadcast_in_dim.15), calls=%async_computation.2 | async-start | bytes 524288 | tf_op jit(solution)/shard_map/all_to_all | solution.py:211
  52.6 6.7 %collective-permute-done.1.refs_9_ = f32[1024,512]{1,0:T(8,128)S(1)} collective-permute-done((f32[1024,512]{1,0:T(8,128)}, f32[1024,512]{1,0:T(8,128)S(1)}, u32[]{:S(2)}, u32[]{:S(2)}) %collective-permute-start.1) | collective-permute-done | bytes 2097184 | tf_op jit(solution)/shard_map/ppermute | solution.py:198
  59.3 0.0 copy-start.1
  59.3 1.1 slice.18
  60.4 0.0 collective-permute-start.2
  60.4 0.0 collective-permute-done.3.refs_10_
  60.4 2.3 %slice.19 = f32[512,512]{1,0:T(8,128)} slice(f32[1024,512]{1,0:T(8,128)} %collective-permute-done.3.refs_10_), slice={[512:1024], [0:512]} | slice | bytes 2097152 | tf_op jit(solution)/shard_map/slice | solution.py:219
  62.7 0.0 copy-done.1
  62.7 2.7 %collective-permute-start.4 = (f32[512,512]{1,0:T(8,128)}, f32[512,512]{1,0:T(8,128)}, u32[]{:S(2)}, u32[]{:S(2)}) collective-permute-start(f32[512,512]{1,0:T(8,128)} %slice.19), channel_id=1, source_target_pairs={{0,3},{1,0},{2,1},{3,2},{4,7},{5,4},{6,5},{7,6},{8,11},{9,8},{10,9... | collective-permute-start | bytes 3145736 | tf_op jit(solution)/shard_map/ppermute | solution.py:201
  65.3 0.0 all-to-all-done.2
  65.3 1.1 broadcast_in_dim.17
  66.4 3.5 %all-to-all-start.3 = ((f32[4,128,512]{2,1,0:T(8,128)}), f32[4,128,512]{2,1,0:T(8,128)S(1)}, u32[]{:S(2)}, u32[]{:S(2)}) async-start(f32[4,128,512]{2,1,0:T(8,128)} %broadcast_in_dim.17), calls=%async_computation.3 | async-start | bytes 2097152 | tf_op jit(solution)/shard_map/all_to_all | solution.py:211
  70.0 15.8 %collective-permute-done.2.refs_11_ = f32[512,512]{1,0:T(8,128)S(1)} collective-permute-done((f32[512,512]{1,0:T(8,128)}, f32[512,512]{1,0:T(8,128)S(1)}, u32[]{:S(2)}, u32[]{:S(2)}) %collective-permute-start.2) | collective-permute-done | bytes 1048608 | tf_op jit(solution)/shard_map/ppermute | solution.py:198
  85.7 0.0 copy-start.2
  85.7 1.3 %collective-permute-done.4.refs_12_ = f32[512,512]{1,0:T(8,128)} collective-permute-done((f32[512,512]{1,0:T(8,128)}, f32[512,512]{1,0:T(8,128)}, u32[]{:S(2)}, u32[]{:S(2)}) %collective-permute-start.4) | collective-permute-done | bytes 1048608 | tf_op jit(solution)/shard_map/ppermute | solution.py:201
  87.0 0.0 all-to-all-done.3
  87.0 0.0 copy-start
  87.0 2.0 %collective-permute-start.8 = (f32[512,512]{1,0:T(8,128)S(1)}, f32[512,512]{1,0:T(8,128)S(1)}, u32[]{:S(2)}, u32[]{:S(2)}) collective-permute-start(f32[512,512]{1,0:T(8,128)S(1)} %bitcast.20), channel_id=1, source_target_pairs={{0,4},{4,0},{8,12},{12,8},{16,20},{20,16},{24,28},{28,24},{32,36},... | collective-permute-start | bytes 3145736 | tf_op jit(solution)/shard_map/ppermute | solution.py:195
  89.0 0.6 pad_add_fusion.at_ref
  89.6 0.9 constant_dynamic-slice_fusion
  90.5 1.9 %collective-permute-start.7 = (f32[128,512]{1,0:T(8,128)}, f32[128,512]{1,0:T(8,128)S(1)}, u32[]{:S(2)}, u32[]{:S(2)}) collective-permute-start(f32[128,512]{1,0:T(8,128)} %get-tuple-element.20), channel_id=1, source_target_pairs={{0,2},{1,3},{2,0},{3,1},{4,6},{5,7},{6,4},{7,5},{8,10},{9,11},{10,... | collective-permute-start | bytes 786440 | tf_op jit(solution)/shard_map/ppermute | solution.py:228
  92.4 1.5 %collective-permute-start.6 = (f32[128,512]{1,0:T(8,128)}, f32[128,512]{1,0:T(8,128)S(1)}, u32[]{:S(2)}, u32[]{:S(2)}) collective-permute-start(f32[128,512]{1,0:T(8,128)} %get-tuple-element.21), channel_id=1, source_target_pairs={{0,3},{1,0},{2,1},{3,2},{4,7},{5,4},{6,5},{7,6},{8,11},{9,8},{10,9... | collective-permute-start | bytes 786440 | tf_op jit(solution)/shard_map/ppermute | solution.py:201
  93.9 0.6 collective-permute-start.5
  94.5 0.0 collective-permute-done.8
  94.5 0.0 copy-start.3
  94.5 0.0 copy-done
  94.5 1.1 copy-done.3
  95.6 8.8 %shard_map.60 = f32[1024,512]{1,0:T(8,128)} custom-call(s32[3]{0:T(128)} %pad_add_fusion.at_ref, f32[1024,512]{1,0:T(8,128)} %cot_ref.3, f32[1024,1024]{1,0:T(8,128)} %panel_ref.3, f32[4,2,64,512]{3,2,1,0:T(8,128)} %bitcast.22, f32[4,2,64,512]{3,2,1,0:T(8,128)} %bitcast.25), custom_call_target="tpu_custom_call" | custom-call | flops 3221225472 | bytes 10485760 | tf_op jit(solution)/shard_map/pallas_call | solution.py:106
  104.4 0.0 copy-done.2
  104.4 0.0 collective-permute-done.7
  104.4 0.0 copy-start.4
  104.4 2.3 %collective-permute-done.6 = f32[128,512]{1,0:T(8,128)S(1)} collective-permute-done((f32[128,512]{1,0:T(8,128)}, f32[128,512]{1,0:T(8,128)S(1)}, u32[]{:S(2)}, u32[]{:S(2)}) %collective-permute-start.6) | collective-permute-done | bytes 262176 | tf_op jit(solution)/shard_map/ppermute | solution.py:201
  106.6 0.0 copy-start.5
  106.6 0.0 collective-permute-done.5
  106.6 0.0 copy-start.6
  106.6 1.1 collective-permute-start.9
  107.7 0.1 collective-permute-start.10
  107.8 0.4 collective-permute-start.11
  108.2 0.7 collective-permute-done.9
  108.9 0.0 copy-start.7
  108.9 0.4 collective-permute-done.10
  109.3 0.0 copy-start.8
  109.3 0.4 collective-permute-done.11
  109.6 0.0 copy-start.9
  109.6 0.0 copy-done.4
  109.6 0.0 copy-done.5
  109.6 0.0 copy-done.6
  109.6 0.0 copy-done.7
  109.7 0.3 copy-done.8
  110.0 0.4 copy-done.9
  110.3 9.0 %shard_map.61 = f32[2,128,1024]{2,1,0:T(8,128)} custom-call(s32[3]{0:T(128)} %pad_add_fusion.at_ref, f32[4,2,64,512]{3,2,1,0:T(8,128)} %bitcast.23, f32[4,2,64,512]{3,2,1,0:T(8,128)} %bitcast.26, f32[1,2,64,512]{3,2,1,0:T(8,128)} %bitcast.31, f32[1,2,64,512]{3,2,1,0:T(8,128)} %bitcast.32, f32[1,2,64,512]{3,2,1,0:T(8,128)} %bitcast.30, ...), custom_call_target="tpu_custom_call" | custom-call | flops 3221225472 | bytes 12582912 | tf_op jit(solution)/shard_map/pallas_call | solution.py:170
  (2 shorter events, 0.0 us)
Async XLA Ops:
  7.3 5.9 %collective-permute-start = (f32[512,512]{1,0:T(8,128)}, f32[512,512]{1,0:T(8,128)S(1)}, u32[]{:S(2)}, u32[]{:S(2)}) collective-permute-start(f32[512,512]{1,0:T(8,128)} %bitcast.35), channel_id=1, source_target_pairs={{0,4},{4,0},{8,12},{12,8},{16,20},{20,16},{24,28},{28,24},{32,36},... | collective-permute-start | bytes 3145736 | tf_op jit(solution)/shard_map/ppermute | solution.py:195
  10.6 48.7 %collective-permute-start.1 = (f32[1024,512]{1,0:T(8,128)}, f32[1024,512]{1,0:T(8,128)S(1)}, u32[]{:S(2)}, u32[]{:S(2)}) collective-permute-start(f32[1024,512]{1,0:T(8,128)} %refs_8_.1), channel_id=1, source_target_pairs={{0,1},{1,2},{2,3},{3,0},{4,5},{5,6},{6,7},{7,4},{8,9},{9,10},{10,1... | collective-permute-start | bytes 6291464 | tf_op jit(solution)/shard_map/ppermute | solution.py:198
  10.6 49.8 %collective-permute-start.3 = (f32[1024,512]{1,0:T(8,128)}, f32[1024,512]{1,0:T(8,128)}, u32[]{:S(2)}, u32[]{:S(2)}) collective-permute-start(f32[1024,512]{1,0:T(8,128)} %refs_8_.1), channel_id=1, source_target_pairs={{0,3},{1,0},{2,1},{3,2},{4,7},{5,4},{6,5},{7,6},{8,11},{9,8},{10,9... | collective-permute-start | bytes 6291464 | tf_op jit(solution)/shard_map/ppermute | solution.py:201
  49.2 16.1 %all-to-all-start.2 = ((f32[8,16,512]{2,1,0:T(8,128)}), f32[8,16,512]{2,1,0:T(8,128)S(1)}, u32[]{:S(2)}, u32[]{:S(2)}) async-start(f32[8,16,512]{2,1,0:T(8,128)} %broadcast_in_dim.15), calls=%async_computation.2 | async-start | bytes 524288 | tf_op jit(solution)/shard_map/all_to_all | solution.py:211
  59.3 3.4 %copy-start.1 = (f32[1024,512]{1,0:T(8,128)}, f32[1024,512]{1,0:T(8,128)S(1)}, u32[]{:S(2)}) copy-start(f32[1024,512]{1,0:T(8,128)S(1)} %collective-permute-done.1.refs_9_) | copy-start | bytes 6291460
  60.4 25.3 %collective-permute-start.2 = (f32[512,512]{1,0:T(8,128)}, f32[512,512]{1,0:T(8,128)S(1)}, u32[]{:S(2)}, u32[]{:S(2)}) collective-permute-start(f32[512,512]{1,0:T(8,128)} %slice.18), channel_id=1, source_target_pairs={{0,1},{1,2},{2,3},{3,0},{4,5},{5,6},{6,7},{7,4},{8,9},{9,10},{10,1... | collective-permute-start | bytes 3145736 | tf_op jit(solution)/shard_map/ppermute | solution.py:198
  62.7 24.4 %collective-permute-start.4 = (f32[512,512]{1,0:T(8,128)}, f32[512,512]{1,0:T(8,128)}, u32[]{:S(2)}, u32[]{:S(2)}) collective-permute-start(f32[512,512]{1,0:T(8,128)} %slice.19), channel_id=1, source_target_pairs={{0,3},{1,0},{2,1},{3,2},{4,7},{5,4},{6,5},{7,6},{8,11},{9,8},{10,9... | collective-permute-start | bytes 3145736 | tf_op jit(solution)/shard_map/ppermute | solution.py:201
  66.4 20.6 %all-to-all-start.3 = ((f32[4,128,512]{2,1,0:T(8,128)}), f32[4,128,512]{2,1,0:T(8,128)S(1)}, u32[]{:S(2)}, u32[]{:S(2)}) async-start(f32[4,128,512]{2,1,0:T(8,128)} %broadcast_in_dim.17), calls=%async_computation.3 | async-start | bytes 2097152 | tf_op jit(solution)/shard_map/all_to_all | solution.py:211
  85.7 18.7 %copy-start.2 = (f32[512,512]{1,0:T(8,128)}, f32[512,512]{1,0:T(8,128)S(1)}, u32[]{:S(2)}) copy-start(f32[512,512]{1,0:T(8,128)S(1)} %collective-permute-done.2.refs_11_) | copy-start | bytes 3145732
  87.0 7.5 %copy-start = (f32[4,128,512]{2,1,0:T(8,128)}, f32[4,128,512]{2,1,0:T(8,128)S(1)}, u32[]{:S(2)}) copy-start(f32[4,128,512]{2,1,0:T(8,128)S(1)} %all-to-all-done.3) | copy-start | bytes 3145732
  87.0 7.5 %collective-permute-start.8 = (f32[512,512]{1,0:T(8,128)S(1)}, f32[512,512]{1,0:T(8,128)S(1)}, u32[]{:S(2)}, u32[]{:S(2)}) collective-permute-start(f32[512,512]{1,0:T(8,128)S(1)} %bitcast.20), channel_id=1, source_target_pairs={{0,4},{4,0},{8,12},{12,8},{16,20},{20,16},{24,28},{28,24},{32,36},... | collective-permute-start | bytes 3145736 | tf_op jit(solution)/shard_map/ppermute | solution.py:195
  90.5 13.9 %collective-permute-start.7 = (f32[128,512]{1,0:T(8,128)}, f32[128,512]{1,0:T(8,128)S(1)}, u32[]{:S(2)}, u32[]{:S(2)}) collective-permute-start(f32[128,512]{1,0:T(8,128)} %get-tuple-element.20), channel_id=1, source_target_pairs={{0,2},{1,3},{2,0},{3,1},{4,6},{5,7},{6,4},{7,5},{8,10},{9,11},{10,... | collective-permute-start | bytes 786440 | tf_op jit(solution)/shard_map/ppermute | solution.py:228
  92.4 14.2 %collective-permute-start.6 = (f32[128,512]{1,0:T(8,128)}, f32[128,512]{1,0:T(8,128)S(1)}, u32[]{:S(2)}, u32[]{:S(2)}) collective-permute-start(f32[128,512]{1,0:T(8,128)} %get-tuple-element.21), channel_id=1, source_target_pairs={{0,3},{1,0},{2,1},{3,2},{4,7},{5,4},{6,5},{7,6},{8,11},{9,8},{10,9... | collective-permute-start | bytes 786440 | tf_op jit(solution)/shard_map/ppermute | solution.py:201
  93.9 12.7 %collective-permute-start.5 = (f32[128,512]{1,0:T(8,128)}, f32[128,512]{1,0:T(8,128)S(1)}, u32[]{:S(2)}, u32[]{:S(2)}) collective-permute-start(f32[128,512]{1,0:T(8,128)} %get-tuple-element.22), channel_id=1, source_target_pairs={{0,1},{1,2},{2,3},{3,0},{4,5},{5,6},{6,7},{7,4},{8,9},{9,10},{10,1... | collective-permute-start | bytes 786440 | tf_op jit(solution)/shard_map/ppermute | solution.py:198
  94.5 1.1 copy-start.3
  104.4 5.3 %copy-start.4 = (f32[128,512]{1,0:T(8,128)}, f32[128,512]{1,0:T(8,128)S(1)}, u32[]{:S(2)}) copy-start(f32[128,512]{1,0:T(8,128)S(1)} %collective-permute-done.7) | copy-start | bytes 786436
  106.6 3.0 %copy-start.5 = (f32[128,512]{1,0:T(8,128)}, f32[128,512]{1,0:T(8,128)S(1)}, u32[]{:S(2)}) copy-start(f32[128,512]{1,0:T(8,128)S(1)} %collective-permute-done.6) | copy-start | bytes 786436
  106.6 3.0 %copy-start.6 = (f32[128,512]{1,0:T(8,128)}, f32[128,512]{1,0:T(8,128)S(1)}, u32[]{:S(2)}) copy-start(f32[128,512]{1,0:T(8,128)S(1)} %collective-permute-done.5) | copy-start | bytes 786436
  106.6 2.2 %collective-permute-start.9 = (f32[128,512]{1,0:T(8,128)S(1)}, f32[128,512]{1,0:T(8,128)S(1)}, u32[]{:S(2)}, u32[]{:S(2)}) collective-permute-start(f32[128,512]{1,0:T(8,128)S(1)} %collective-permute-done.5), channel_id=1, source_target_pairs={{0,4},{4,0},{8,12},{12,8},{16,20},{20,16},{24,28},{28,24},{32,36},... | collective-permute-start | bytes 786440 | tf_op jit(solution)/shard_map/ppermute | solution.py:195
  107.7 1.5 %collective-permute-start.10 = (f32[128,512]{1,0:T(8,128)S(1)}, f32[128,512]{1,0:T(8,128)S(1)}, u32[]{:S(2)}, u32[]{:S(2)}) collective-permute-start(f32[128,512]{1,0:T(8,128)S(1)} %collective-permute-done.6), channel_id=1, source_target_pairs={{0,4},{4,0},{8,12},{12,8},{16,20},{20,16},{24,28},{28,24},{32,36},... | collective-permute-start | bytes 786440 | tf_op jit(solution)/shard_map/ppermute | solution.py:195
  107.8 1.8 %collective-permute-start.11 = (f32[128,512]{1,0:T(8,128)S(1)}, f32[128,512]{1,0:T(8,128)S(1)}, u32[]{:S(2)}, u32[]{:S(2)}) collective-permute-start(f32[128,512]{1,0:T(8,128)S(1)} %collective-permute-done.7), channel_id=1, source_target_pairs={{0,4},{4,0},{8,12},{12,8},{16,20},{20,16},{24,28},{28,24},{32,36},... | collective-permute-start | bytes 786440 | tf_op jit(solution)/shard_map/ppermute | solution.py:195
  108.9 0.8 copy-start.7
  109.3 0.7 copy-start.8
  109.6 0.7 copy-start.9
